TPU v7x, 256 devices: a whole 4x4x8 slice. The times are simulated.
256 devices in a mesh: depth: 16 (over y, x_lo, core), height: 16 (over z, x_hi).
Axes of the slice: x: 4 (x_hi: 2, x_lo: 2; x = x_hi * 2 + x_lo), y: 4, z: 8, core: 2. Of those that a mesh axis runs over, the one named last changes fastest.
Arguments:
- bottom: bfloat16 [16, 16, 32, 320], P('depth', None, None, 'height'), may hold values from -6 to 6
- skip: bfloat16 [32, 32, 64, 128], P('depth', 'height'), may hold values from -6 to 6
- upconv_kernel: bfloat16 [3, 3, 3, 320, 128], replicated, may hold values from -0.1875 to 0.1875
- w_first: bfloat16 [3, 3, 3, 256, 128], replicated, may hold values from -0.078125 to 0.078125
- w_second: bfloat16 [3, 3, 3, 128, 128], replicated, may hold values from -0.109375 to 0.109375
- cotangent: bfloat16 [32, 32, 64, 128], P('depth', 'height'), may hold values from -6 to 6
Outputs:
- result: bfloat16 [32, 32, 64, 128], P('depth', 'height')
- coarse_input_gradient: bfloat16 [16, 16, 32, 320], P('depth', None, None, 'height')
- grad_skip: bfloat16 [32, 32, 64, 128], P('depth', 'height')
- g_up: float32 [3, 3, 3, 320, 128], P(None, None, None, 'height', 'depth')
- g_first: float32 [3, 3, 3, 256, 128], P(None, None, None, 'height', 'depth')
- g_second: float32 [3, 3, 3, 128, 128], P(None, None, None, 'height', 'depth')
All inputs are finite; a program needn't handle non-finite values.
Results may differ from a plain program's by a relative error of at most 0.015.
Values may be sent and summed in bfloat16 or wider, within the bound.
A program may use at most 192 MiB of HBM per device.

v0:
```python
import math

import jax
import jax.numpy as jnp
from jax import lax
from jax.sharding import PartitionSpec as P

TAP_TABLE = (((1, 0),), ((2, 0), (0, 1)))


def extended(x, sides, width):
    for axis, dim in sides:
        peers, length = (lax.axis_size(axis), x.shape[dim])
        up = [(i, (i + 1) % peers) for i in range(peers - 1)]
        down = [(j, i) for i, j in up]
        last = lax.slice_in_dim(x, length - width, length, axis=dim)
        leading = lax.slice_in_dim(x, 0, width, axis=dim)
        before = lax.ppermute(last, axis, up)
        after = lax.ppermute(leading, axis, down)
        x = jnp.concatenate([before, x, after], axis=dim)
    return x


def from_behind(block, axis, distance):
    devices = range(lax.axis_size(axis))
    route = [(i - distance, i) for i in devices if i - distance in devices]
    return lax.ppermute(block, axis, route)


def upsample(widened_volume, weight_tensor):
    coarse = (widened_volume.shape[0] - 1, widened_volume.shape[1] - 1, widened_volume.shape[2] - 1)
    chans = widened_volume.shape[3]
    outer = []
    for phase_d in range(2):
        middle = []
        for phase_h in range(2):
            inner = []
            for phase_w in range(2):
                summed = None
                for tap_d, shift_d in TAP_TABLE[phase_d]:
                    for tap_h, shift_h in TAP_TABLE[phase_h]:
                        for tap_w, shift_w in TAP_TABLE[phase_w]:
                            sliced = widened_volume[
                                shift_d : shift_d + coarse[0],
                                shift_h : shift_h + coarse[1],
                                shift_w : shift_w + coarse[2],
                            ]
                            product = jnp.dot(
                                sliced.reshape(-1, chans),
                                weight_tensor[tap_d, tap_h, tap_w],
                                preferred_element_type=jnp.float32,
                            )
                            summed = product if summed is None else summed + product
                inner.append(summed)
            middle.append(jnp.stack(inner))
        outer.append(jnp.stack(middle))
    outc = weight_tensor.shape[4]
    stacked = jnp.stack(outer).reshape(2, 2, 2, coarse[0], coarse[1], coarse[2], outc)
    stacked = stacked.transpose(3, 0, 4, 1, 5, 2, 6)
    return stacked.reshape(2 * coarse[0], 2 * coarse[1], 2 * coarse[2], outc)


def reduce_resolution(widened_volume, weight_tensor):
    coarse = (
        (widened_volume.shape[0] - 1) // 2,
        (widened_volume.shape[1] - 1) // 2,
        (widened_volume.shape[2] - 1) // 2,
    )
    chans = widened_volume.shape[3]
    summed = None
    for tap_d in range(3):
        for tap_h in range(3):
            for tap_w in range(3):
                sliced = widened_volume[
                    tap_d : tap_d + 2 * coarse[0] : 2,
                    tap_h : tap_h + 2 * coarse[1] : 2,
                    tap_w : tap_w + 2 * coarse[2] : 2,
                ]
                product = lax.dot_general(
                    sliced.reshape(-1, chans),
                    weight_tensor[tap_d, tap_h, tap_w],
                    (((1,), (1,)), ((), ())),
                    preferred_element_type=jnp.float32,
                )
                summed = product if summed is None else summed + product
    return summed.reshape(coarse + (weight_tensor.shape[3],))


def up_weight_grad(coarse_in, widened_volume):
    shape = coarse_in.shape
    flat_in = coarse_in.reshape(-1, shape[3])
    listed = []
    for tap_d in range(3):
        for tap_h in range(3):
            for tap_w in range(3):
                sliced = widened_volume[
                    tap_d : tap_d + 2 * shape[0] : 2,
                    tap_h : tap_h + 2 * shape[1] : 2,
                    tap_w : tap_w + 2 * shape[2] : 2,
                ]
                listed.append(
                    lax.dot_general(
                        flat_in,
                        sliced.reshape(-1, widened_volume.shape[3]),
                        (((0,), (0,)), ((), ())),
                        preferred_element_type=jnp.float32,
                    )
                )
    return jnp.stack(listed).reshape(3, 3, 3, shape[3], widened_volume.shape[3])


def conv_same(padded, weight_tensor):
    cells = (padded.shape[0] - 2, padded.shape[1] - 2, padded.shape[2] - 2)
    chans = padded.shape[3]
    summed = None
    for tap_d in range(3):
        for tap_h in range(3):
            for tap_w in range(3):
                sliced = padded[
                    tap_d : tap_d + cells[0], tap_h : tap_h + cells[1], tap_w : tap_w + cells[2]
                ]
                product = jnp.dot(
                    sliced.reshape(-1, chans),
                    weight_tensor[tap_d, tap_h, tap_w],
                    preferred_element_type=jnp.float32,
                )
                summed = product if summed is None else summed + product
    return summed.reshape(cells + (weight_tensor.shape[4],))


def conv_back(padded, weight_tensor):
    cells = (padded.shape[0] - 2, padded.shape[1] - 2, padded.shape[2] - 2)
    chans = padded.shape[3]
    summed = None
    for tap_d in range(3):
        for tap_h in range(3):
            for tap_w in range(3):
                sliced = padded[
                    2 - tap_d : 2 - tap_d + cells[0],
                    2 - tap_h : 2 - tap_h + cells[1],
                    2 - tap_w : 2 - tap_w + cells[2],
                ]
                product = lax.dot_general(
                    sliced.reshape(-1, chans),
                    weight_tensor[tap_d, tap_h, tap_w],
                    (((1,), (1,)), ((), ())),
                    preferred_element_type=jnp.float32,
                )
                summed = product if summed is None else summed + product
    return summed.reshape(cells + (weight_tensor.shape[3],))


def conv_weight(padded, error):
    cells = error.shape[:3]
    flat_err = error.reshape(-1, error.shape[3])
    listed = []
    for tap_d in range(3):
        for tap_h in range(3):
            for tap_w in range(3):
                sliced = padded[
                    tap_d : tap_d + cells[0], tap_h : tap_h + cells[1], tap_w : tap_w + cells[2]
                ]
                listed.append(
                    lax.dot_general(
                        sliced.reshape(-1, padded.shape[3]),
                        flat_err,
                        (((0,), (0,)), ((), ())),
                        preferred_element_type=jnp.float32,
                    )
                )
    return jnp.stack(listed).reshape(3, 3, 3, padded.shape[3], error.shape[3])


def slope(values):
    sig = jax.nn.sigmoid(values)
    return sig * (1.0 + values * (1.0 - sig))


def surround(field):
    padded = extended(field, (("depth", 0), ("height", 1)), 1)
    return jnp.pad(padded, ((0, 0), (0, 0), (1, 1), (0, 0)))


def per_device(bottom, skip, upconv_kernel, w_first, w_second, cotangent):
    depths = lax.axis_size("depth")
    groups = lax.axis_size("height")
    cells = skip.shape[:3]
    factor = 1.0 / math.sqrt(cells[0] * depths * cells[1] * groups * cells[2])
    up_chans = upconv_kernel.shape[4]
    block = lax.all_to_all(bottom, "height", split_axis=1, concat_axis=3, tiled=True)
    plane_next = from_behind(block, "depth", -1)
    widened_volume = jnp.concatenate([block, plane_next], 0)
    row_next = from_behind(widened_volume, "height", -1)
    widened_volume = jnp.concatenate([widened_volume, row_next], 1)
    widened_volume = jnp.pad(widened_volume, ((0, 0), (0, 0), (0, 1), (0, 0)))
    upsampled = upsample(widened_volume, upconv_kernel).astype(jnp.bfloat16)
    joined = jnp.concatenate([upsampled, skip], 3)
    joined_pad = surround(joined)
    first_pre = conv_same(joined_pad, w_first)
    hidden = jax.nn.silu(first_pre).astype(jnp.bfloat16)
    hidden_pad = surround(hidden)
    second_pre = conv_same(hidden_pad, w_second)
    result = jax.nn.silu(second_pre).astype(jnp.bfloat16)
    err_second = (cotangent.astype(jnp.float32) * slope(second_pre)).astype(jnp.bfloat16)
    g_second_local = conv_weight(hidden_pad, err_second) * factor
    back_hidden = conv_back(surround(err_second), w_second)
    err_first = (back_hidden * slope(first_pre)).astype(jnp.bfloat16)
    g_first_local = conv_weight(joined_pad, err_first) * factor
    back_joined = conv_back(surround(err_first), w_first)
    back_up = back_joined[..., :up_chans].astype(jnp.bfloat16)
    grad_skip = back_joined[..., up_chans:].astype(jnp.bfloat16)
    plane_prev = from_behind(back_up[-1:], "depth", 1)
    lower_level = jnp.concatenate([plane_prev, back_up], 0)
    row_prev = from_behind(lower_level[:, -1:], "height", 1)
    lower_level = jnp.concatenate([row_prev, lower_level], 1)
    lower_level = jnp.pad(lower_level, ((0, 0), (0, 0), (1, 0), (0, 0)))
    block_gradient = reduce_resolution(lower_level, upconv_kernel).astype(jnp.bfloat16)
    coarse_input_gradient = lax.all_to_all(
        block_gradient, "height", split_axis=3, concat_axis=1, tiled=True
    )
    g_up_part = lax.psum_scatter(
        up_weight_grad(block, lower_level) * factor, "height", scatter_dimension=3, tiled=True
    )
    g_up = lax.psum_scatter(g_up_part, "depth", scatter_dimension=4, tiled=True)
    part_first, part_second = (
        lax.psum_scatter(g_first_local, "depth", scatter_dimension=4, tiled=True),
        lax.psum_scatter(g_second_local, "depth", scatter_dimension=4, tiled=True),
    )
    g_first, g_second = (
        lax.psum_scatter(part_first, "height", scatter_dimension=3, tiled=True),
        lax.psum_scatter(part_second, "height", scatter_dimension=3, tiled=True),
    )
    return (result, coarse_input_gradient, grad_skip, g_up, g_first, g_second)


def solution(mesh):
    return jax.shard_map(
        per_device,
        mesh=mesh,
        in_specs=(
            P("depth", None, None, "height"),
            P("depth", "height", None, None),
            P(),
            P(),
            P(),
            P("depth", "height", None, None),
        ),
        out_specs=(
            P("depth", "height", None, None),
            P("depth", None, None, "height"),
            P("depth", "height", None, None),
            P(None, None, None, "height", "depth"),
            P(None, None, None, "height", "depth"),
            P(None, None, None, "height", "depth"),
        ),
        check_vma=False,
    )
```

profile of v0, /device:TPU:1, one launch (start us, length us, event | category | flops | bytes accessed | tf_op | source)
XLA Modules:
  0.0 1108.7 jit_solution(6268784375122876979)
XLA Ops:
  8.4 20.3 %all_to_all.36 = bf16[16,2,320]{2,1,0:T(2,128)(2,1)S(1)} all-to-all(bf16[16,2,320]{2,1,0:T(2,128)(2,1)S(1)} %reshape.778), channel_id=1, replica_groups=mesh['depth'=16,'height'=16] {'height'}, dimensions={0} | all-to-all | bytes 40960 | tf_op jit(solution)/shard_map/all_to_all | solution.py:190
  36.6 4.0 collective-permute-start
  40.8 1.5 collective-permute-done
  42.4 1.3 collective-permute-start.1
  43.8 5.6 collective-permute-done.1
  52.2 2.3 collective-permute-start.3
  54.5 3.3 collective-permute-start.2
  57.7 1.3 collective-permute-done.2
  59.1 1.3 collective-permute-start.5
  60.4 5.5 collective-permute-start.4
  66.9 1.8 collective-permute-done.4
  76.0 1.9 collective-permute-start.7
  77.9 5.1 collective-permute-start.6
  84.4 1.4 collective-permute-start.9
  85.8 6.9 collective-permute-start.8
  92.8 1.3 collective-permute-done.8
  99.5 1.9 collective-permute-start.11
  101.5 4.8 collective-permute-start.10
  111.2 1.3 collective-permute-start.13
  112.5 7.0 collective-permute-start.12
  119.5 1.3 collective-permute-done.12
  125.9 1.9 collective-permute-start.15
  127.9 3.8 collective-permute-start.14
  132.7 1.3 collective-permute-start.17
  134.0 6.8 collective-permute-start.16
  140.8 1.2 collective-permute-done.16
  147.8 4.4 collective-permute-start.18
  153.2 7.1 collective-permute-start.19
  160.4 1.2 copy-done.4
  162.3 1.3 slice.1229
  188.2 5.5 copy.39
  193.8 2.9 broadcast_multiply_fusion.2
  196.7 4.0 copy.42
  217.6 258.9 %all-reduce.13.cloned.1.call-done = f32[3,3,3,320,128]{4,2,1,0,3:T(4,128)} async-done(((f32[3,3,3,320,128]{4,2,1,0,3:T(4,128)}), f32[3,3,3,320,128]{4,2,1,0,3:T(4,128)}) %all-reduce.13.cloned.1.call-update) | async-done | bytes 4423696
  476.5 1.8 constant_dynamic-slice_fusion.2
  478.3 3.5 copy.40
  488.9 4.1 broadcast_multiply_fusion.1
  493.0 5.2 copy.41
  503.8 123.0 %all-reduce.15.cloned.1.call-done = (f32[3,3,3,20,128]{3,2,1,0,4:T(4,128)}, f32[3,3,3,128,128]{3,2,1,0,4:T(4,128)}) async-done(((f32[3,3,3,20,128]{3,2,1,0,4:T(4,128)}, f32[3,3,3,128,128]{3,2,1,0,4:T(4,128)}), (f32[3,3,3,20,128]{3,2,1,0,4:T(4,128)}, f32[3,3,3,128,128]{3,2,1,0,4:T(4,128)})) %all-reduce.15.cloned.1.call-update) | async-done | bytes 2045968
  627.8 4.9 copy.104
  632.7 6.6 reshape.773
  639.5 59.6 %reduce-scatter.8.cloned.1.call-done = f32[3,3,3,256,8]{3,4,2,1,0:T(8,128)} async-done(((f32[3,3,3,256,128]{3,4,2,1,0:T(8,128)}), f32[3,3,3,256,8]{3,4,2,1,0:T(8,128)}) %reduce-scatter.8.cloned.1.call-update) | async-done | bytes 221200 | tf_op jit(solution)/shard_map/reduce_scatter | solution.py:226
  699.1 5.2 copy.102
  704.3 5.4 reshape.771
  712.0 17.7 %all_to_all.37 = bf16[16,2,320]{2,1,0:T(2,128)(2,1)S(1)} all-to-all(bf16[16,2,320]{2,1,0:T(2,128)(2,1)S(1)} %reshape.780), channel_id=1, replica_groups=mesh['depth'=16,'height'=16] {'height'}, dimensions={0} | all-to-all | bytes 40960 | tf_op jit(solution)/shard_map/all_to_all | solution.py:218
  732.5 166.4 %reduce-scatter.12.cloned.1.call-done = f32[8,216]{1,0:T(8,128)} async-done(((f32[128,216]{1,0:T(8,128)}), f32[8,216]{1,0:T(8,128)}) %reduce-scatter.12.cloned.1.call-update) | async-done | bytes 6928
  900.0 1.1 copy.45
  901.2 199.3 %reduce-scatter.10.cloned.1.call-done = f32[16,216]{1,0:T(8,128)} async-done(((f32[256,216]{1,0:T(8,128)}), f32[16,216]{1,0:T(8,128)}) %reduce-scatter.10.cloned.1.call-update) | async-done | bytes 13840
  (462 shorter events, 106.1 us)
Async XLA Ops:
  7.2 33.5 %copy-start = (bf16[3,3,3,320,128]{4,3,2,1,0:T(8,128)(2,1)S(1)}, bf16[3,3,3,320,128]{4,3,2,1,0:T(8,128)(2,1)}, u32[]{:S(2)}) copy-start(bf16[3,3,3,320,128]{4,3,2,1,0:T(8,128)(2,1)} %param.8) | copy-start | bytes 6635524
  7.2 469.3 %all-reduce.13.cloned.1.call-start = ((), (), s32[]{:S(2)}) async-start(), calls=%async_computation.8 | async-start | bytes 11796480
  32.2 19.9 %copy-start.5 = (bf16[2,2,64,128]{3,2,1,0:T(8,128)(2,1)S(1)}, bf16[2,2,64,128]{3,2,1,0:T(8,128)(2,1)}, u32[]{:S(2)}) copy-start(bf16[2,2,64,128]{3,2,1,0:T(8,128)(2,1)} %param.7) | copy-start | bytes 196612
  36.6 5.7 collective-permute-start
  42.4 7.0 collective-permute-start.1
  52.2 5.6 collective-permute-start.3
  54.5 4.6 collective-permute-start.2
  59.1 7.8 collective-permute-start.5
  60.4 8.3 collective-permute-start.4
  73.7 9.3 copy-start.47
  76.0 8.3 collective-permute-start.7
  77.9 6.4 collective-permute-start.6
  84.3 10.1 copy-start.3
  84.3 26.2 %copy-start.8 = (bf16[1,2,64,128]{3,2,1,0:T(8,128)(2,1)}, bf16[1,2,64,128]{3,2,1,0:T(8,128)(2,1)S(1)}, u32[]{:S(2)}) copy-start(bf16[1,2,64,128]{3,2,1,0:T(8,128)(2,1)S(1)} %collective-permute-done.7) | copy-start | bytes 98308
  84.3 25.5 %copy-start.10 = (bf16[1,2,64,128]{3,2,1,0:T(8,128)(2,1)}, bf16[1,2,64,128]{3,2,1,0:T(8,128)(2,1)S(1)}, u32[]{:S(2)}) copy-start(bf16[1,2,64,128]{3,2,1,0:T(8,128)(2,1)S(1)} %collective-permute-done.6) | copy-start | bytes 98308
  84.4 8.4 collective-permute-start.9
  85.8 8.2 collective-permute-start.8
  99.5 11.6 %collective-permute-start.11 = (bf16[1,2,64,128]{3,2,1,0:T(8,128)(2,1)S(1)}, bf16[1,2,64,128]{3,2,1,0:T(8,128)(2,1)S(1)}, u32[]{:S(2)}, u32[]{:S(2)}) collective-permute-start(bf16[1,2,64,128]{3,2,1,0:T(8,128)(2,1)S(1)} %get-tuple-element.154), channel_id=1, source_target_pairs={{16,0},{32,16},{48,32},{64,48},{80,64},{96,80},{112,96},{128,112},... | collective-permute-start | bytes 98312 | tf_op jit(solution)/shard_map/ppermute | solution.py:19
  101.5 9.7 collective-permute-start.10
  111.2 8.4 collective-permute-start.13
  112.5 8.3 collective-permute-start.12
  125.9 5.9 collective-permute-start.15
  127.9 14.6 %copy-start.2 = (bf16[3,3,3,256,128]{4,3,2,1,0:T(8,128)(2,1)S(1)}, bf16[3,3,3,256,128]{4,3,2,1,0:T(8,128)(2,1)}, u32[]{:S(2)}) copy-start(bf16[3,3,3,256,128]{4,3,2,1,0:T(8,128)(2,1)} %param.9) | copy-start | bytes 5308420
  127.9 4.8 collective-permute-start.14
  132.7 8.1 collective-permute-start.17
  134.0 8.1 collective-permute-start.16
  147.8 5.4 collective-permute-start.18
  153.2 8.5 collective-permute-start.19
  164.4 21.6 %copy-start.42 = (bf16[1,1,32,128]{3,2,1,0:T(8,128)(2,1)}, bf16[1,1,32,128]{3,2,1,0:T(8,128)(2,1)S(1)}, u32[]{:S(2)}) copy-start(bf16[1,1,32,128]{3,2,1,0:T(8,128)(2,1)S(1)} %slice.1230) | copy-start | bytes 24580
  165.2 20.8 %copy-start.40 = (bf16[1,1,32,128]{3,2,1,0:T(8,128)(2,1)}, bf16[1,1,32,128]{3,2,1,0:T(8,128)(2,1)S(1)}, u32[]{:S(2)}) copy-start(bf16[1,1,32,128]{3,2,1,0:T(8,128)(2,1)S(1)} %slice.1231) | copy-start | bytes 24580
  165.9 20.1 %copy-start.38 = (bf16[1,1,32,128]{3,2,1,0:T(8,128)(2,1)}, bf16[1,1,32,128]{3,2,1,0:T(8,128)(2,1)S(1)}, u32[]{:S(2)}) copy-start(bf16[1,1,32,128]{3,2,1,0:T(8,128)(2,1)S(1)} %slice.1232) | copy-start | bytes 24580
  166.6 19.4 %copy-start.36 = (bf16[1,1,32,128]{3,2,1,0:T(8,128)(2,1)}, bf16[1,1,32,128]{3,2,1,0:T(8,128)(2,1)S(1)}, u32[]{:S(2)}) copy-start(bf16[1,1,32,128]{3,2,1,0:T(8,128)(2,1)S(1)} %slice.1233) | copy-start | bytes 24580
  167.4 18.8 %copy-start.34 = (bf16[1,1,32,128]{3,2,1,0:T(8,128)(2,1)}, bf16[1,1,32,128]{3,2,1,0:T(8,128)(2,1)S(1)}, u32[]{:S(2)}) copy-start(bf16[1,1,32,128]{3,2,1,0:T(8,128)(2,1)S(1)} %slice.1234) | copy-start | bytes 24580
  168.1 18.0 %copy-start.32 = (bf16[1,1,32,128]{3,2,1,0:T(8,128)(2,1)}, bf16[1,1,32,128]{3,2,1,0:T(8,128)(2,1)S(1)}, u32[]{:S(2)}) copy-start(bf16[1,1,32,128]{3,2,1,0:T(8,128)(2,1)S(1)} %slice.1235) | copy-start | bytes 24580
  168.9 17.3 %copy-start.30 = (bf16[1,1,32,128]{3,2,1,0:T(8,128)(2,1)}, bf16[1,1,32,128]{3,2,1,0:T(8,128)(2,1)S(1)}, u32[]{:S(2)}) copy-start(bf16[1,1,32,128]{3,2,1,0:T(8,128)(2,1)S(1)} %slice.1236) | copy-start | bytes 24580
  169.6 16.6 %copy-start.28 = (bf16[1,1,32,128]{3,2,1,0:T(8,128)(2,1)}, bf16[1,1,32,128]{3,2,1,0:T(8,128)(2,1)S(1)}, u32[]{:S(2)}) copy-start(bf16[1,1,32,128]{3,2,1,0:T(8,128)(2,1)S(1)} %slice.1237) | copy-start | bytes 24580
  170.4 15.8 %copy-start.26 = (bf16[1,1,32,128]{3,2,1,0:T(8,128)(2,1)}, bf16[1,1,32,128]{3,2,1,0:T(8,128)(2,1)S(1)}, u32[]{:S(2)}) copy-start(bf16[1,1,32,128]{3,2,1,0:T(8,128)(2,1)S(1)} %slice.1238) | copy-start | bytes 24580
  171.1 15.1 %copy-start.24 = (bf16[1,1,32,128]{3,2,1,0:T(8,128)(2,1)}, bf16[1,1,32,128]{3,2,1,0:T(8,128)(2,1)S(1)}, u32[]{:S(2)}) copy-start(bf16[1,1,32,128]{3,2,1,0:T(8,128)(2,1)S(1)} %slice.1239) | copy-start | bytes 24580
  171.8 14.4 %copy-start.22 = (bf16[1,1,32,128]{3,2,1,0:T(8,128)(2,1)}, bf16[1,1,32,128]{3,2,1,0:T(8,128)(2,1)S(1)}, u32[]{:S(2)}) copy-start(bf16[1,1,32,128]{3,2,1,0:T(8,128)(2,1)S(1)} %slice.1240) | copy-start | bytes 24580
  172.6 13.6 %copy-start.20 = (bf16[1,1,32,128]{3,2,1,0:T(8,128)(2,1)}, bf16[1,1,32,128]{3,2,1,0:T(8,128)(2,1)S(1)}, u32[]{:S(2)}) copy-start(bf16[1,1,32,128]{3,2,1,0:T(8,128)(2,1)S(1)} %slice.1241) | copy-start | bytes 24580
  173.3 12.9 %copy-start.18 = (bf16[1,1,32,128]{3,2,1,0:T(8,128)(2,1)}, bf16[1,1,32,128]{3,2,1,0:T(8,128)(2,1)S(1)}, u32[]{:S(2)}) copy-start(bf16[1,1,32,128]{3,2,1,0:T(8,128)(2,1)S(1)} %slice.1242) | copy-start | bytes 24580
  174.1 12.2 %copy-start.16 = (bf16[1,1,32,128]{3,2,1,0:T(8,128)(2,1)}, bf16[1,1,32,128]{3,2,1,0:T(8,128)(2,1)S(1)}, u32[]{:S(2)}) copy-start(bf16[1,1,32,128]{3,2,1,0:T(8,128)(2,1)S(1)} %slice.1243) | copy-start | bytes 24580
  174.8 11.4 %copy-start.14 = (bf16[1,1,32,128]{3,2,1,0:T(8,128)(2,1)}, bf16[1,1,32,128]{3,2,1,0:T(8,128)(2,1)S(1)}, u32[]{:S(2)}) copy-start(bf16[1,1,32,128]{3,2,1,0:T(8,128)(2,1)S(1)} %slice.1244) | copy-start | bytes 24580
  175.6 10.7 copy-start.12
  193.7 433.1 %all-reduce.15.cloned.1.call-start = ((), (), s32[]{:S(2)}) async-start(), calls=%async_computation.9 | async-start | bytes 9437184
  481.7 217.3 %reduce-scatter.8.cloned.1.call-start = ((), (), s32[]{:S(2)}) async-start(), calls=%async_computation.5 | async-start | bytes 3760128 | tf_op jit(solution)/shard_map/reduce_scatter | solution.py:226
  498.4 400.6 %reduce-scatter.12.cloned.1.call-start = ((), (), s32[]{:S(2)}) async-start(), calls=%async_computation.7 | async-start | bytes 139264
  639.3 461.2 %reduce-scatter.10.cloned.1.call-start = ((), (), s32[]{:S(2)}) async-start(), calls=%async_computation.6 | async-start | bytes 278528
  (25 other events, 79.6 us)
Sparse Core Ops, SparseCore 0:
  193.8 282.5 all-reduce.12
  481.8 144.9 all-reduce.14
  629.6 69.4 reduce-scatter.7
  703.2 195.7 reduce-scatter.11
  902.6 197.8 reduce-scatter.9
where the time goes:
time: 1120 us; the launch traced here: 1110 us
  waiting for transfers between devices  823 us (73%)
  local copies, waits for them, and re-layouts  79.2 us (7%)
  starting transfers between devices  73.7 us (7%)
  matrix products  66 us (6%)
  blocking collectives  38 us (3%)
  between operations  17.4 us (2%)
    unnamed x9, waiting for transfers between devices  748 us
    reduce_scatter x1, waiting for transfers between devices, per_device(): lax.psum_scatter(g_first_local, 'depth', scatter_dimension=4, tiled=True)  59.6 us
    ppermute x8, starting transfers between devices, extended(): before = lax.ppermute(last, axis, up)  43.2 us
    unnamed x117, local copies, waits for them, and re-layouts  37.1 us
    dot_general x54, matrix products, conv_weight(): lax.dot_general(sliced.reshape(-1, padded.shape[3]), flat_err, (((0,), (0...  29.2 us
  transfers between devices with their start and end apart: 25, of which 15 were waited for; matrix products, arithmetic and copies ran while one was open for 7% of the time, Pallas kernels for 0%

commit v1 on v0

v1 whole, which is shorter than its diff:
```python
import functools
import math

import jax
import jax.numpy as jnp
from jax import lax
from jax.experimental import pallas as pl
from jax.experimental.pallas import tpu as pltpu
from jax.sharding import PartitionSpec as P

MESH = pl.DeviceIdType.MESH
F32 = jnp.float32
BF16 = jnp.bfloat16
GRID9 = [(a, b) for a in range(3) for b in range(3)]
OTHERS = [(a, b) for a in (-1, 0, 1) for b in (-1, 0, 1) if (a, b) != (0, 0)]
NT = (((1,), (1,)), ((), ()))
PARITY_SHIFT = {0: (1, 1), 1: (0, 0), 2: (1, 0)}


def round_up(value, unit):
    return -(-value // unit) * unit


def remote(src, dst, send, recv, target):
    return pltpu.make_async_remote_copy(
        src_ref=src, dst_ref=dst, send_sem=send, recv_sem=recv, device_id=target, device_id_type=MESH
    )


class Spread:
    def __init__(self, me, count, target, source, slot, send, recv):
        self.me, self.count, self.target = me, count, target
        self.source, self.slot, self.send, self.recv = source, slot, send, recv

    def each(self, act):
        def step(j, carry):
            act(j)
            return carry

        lax.fori_loop(1, self.count, step, 0)

    def outgoing(self, j):
        peer = lax.rem(self.me + j, self.count)
        return remote(
            self.source(peer), self.slot(self.me), self.send.at[peer], self.recv.at[self.me], self.target(peer)
        )

    def incoming(self, j):
        peer = lax.rem(self.me + self.count - j, self.count)
        return remote(
            self.source(peer), self.slot(peer), self.send.at[peer], self.recv.at[peer], self.target(peer)
        )

    def start(self):
        self.each(lambda j: self.outgoing(j).start())

    def wait_recv(self):
        self.each(lambda j: self.incoming(j).wait_recv())

    def wait_send(self):
        self.each(lambda j: self.outgoing(j).wait_send())


def shift_rows(value, by, period):
    rows = value.shape[0]
    row = lax.broadcasted_iota(jnp.int32, value.shape, 0) % period
    edge = 0 if by > 0 else period - 1
    return jnp.where(row == edge, 0.0, pltpu.roll(value, by % rows, 0))


def shift_lanes(value, by, period):
    lanes = value.shape[1]
    lane = lax.broadcasted_iota(jnp.int32, value.shape, 1) % period
    edge = 0 if by > 0 else period - 1
    return jnp.where(lane == edge, 0.0, pltpu.roll(value, by % lanes, 1))


def slope(values):
    sig = jax.nn.sigmoid(values)
    return sig * (1.0 + values * (1.0 - sig))


def dot(a, b, dims=(((1,), (0,)), ((), ()))):
    return lax.dot_general(a, b, dims, preferred_element_type=F32)


def body(
    nd, nh, factor,
    bottom, skip, upw_hbm, w1_hbm, w2_hbm, cot_hbm,
    result, cgrad, gskip, gup, gfirst, gsecond,
    upw, w1, w2, cot, brecv, bg, up32, joined, jg, fp, hid, hg, e2, e1, et2s, et2r, et1s, et1r,
    bu32, bu, buts, butr, cgs, cgr, vt0, vt1, acc1, acc2, gs2, gr2, gs1, gr1, gsu, gru,
    ssem, rsem, hs, hr, loc,
):
    d = lax.axis_index("depth")
    h = lax.axis_index("height")
    cb = bottom.shape[3]
    cw = bottom.shape[2]
    cu = upw.shape[2]
    no = cu // nd
    taps = 27

    weights = [
        pltpu.make_async_copy(upw_hbm, upw, loc.at[0]),
        pltpu.make_async_copy(w1_hbm, w1, loc.at[1]),
        pltpu.make_async_copy(w2_hbm, w2, loc.at[2]),
        pltpu.make_async_copy(cot_hbm, cot, loc.at[3]),
    ]
    own_skip = pltpu.make_async_copy(skip, joined.at[pl.ds(1, 2), pl.ds(1, 2), :, pl.ds(cu, cu)], loc.at[4])
    first_row = lambda p: jnp.clip(p - 1, 0, nh - 3)
    own_rows = pltpu.make_async_copy(bottom.at[0, pl.ds(first_row(h), 3)], brecv.at[h], loc.at[5])

    joined[...] = jnp.zeros_like(joined)
    hid[...] = jnp.zeros_like(hid)
    e2[...] = jnp.zeros_like(e2)
    e1[...] = jnp.zeros_like(e1)
    bu[...] = jnp.zeros_like(bu)

    own_rows.start()
    own_skip.start()
    for copy in weights:
        copy.start()

    barrier = pltpu.get_barrier_semaphore()

    def greet_line(count, target):
        def step(j, carry):
            pl.semaphore_signal(barrier, inc=1, device_id=target(j), device_id_type=MESH)
            return carry

        lax.fori_loop(1, count, step, 0)

    greet_line(nh, lambda j: (d, lax.rem(h + j, nh)))
    greet_line(nd, lambda j: (lax.rem(d + j, nd), h))

    def there(dd, dh):
        ok = None
        for pos, step, count in ((d, dd, nd), (h, dh, nh)):
            if step:
                cond = pos > 0 if step < 0 else pos < count - 1
                ok = cond if ok is None else jnp.logical_and(ok, cond)
        return ok

    for dd in (-1, 1):
        for dh in (-1, 1):
            corner = (lax.rem(d + dd + nd, nd), lax.rem(h + dh + nh, nh))
            pl.semaphore_signal(barrier, inc=1, device_id=corner, device_id_type=MESH)
    pl.semaphore_wait(barrier, nd + nh + 2)

    def src_part(step):
        return {0: pl.ds(1, 2), 1: pl.ds(2, 1), -1: pl.ds(1, 1)}[step]

    def own_part(step):
        return {0: pl.ds(0, 2), 1: pl.ds(1, 1), -1: pl.ds(0, 1)}[step]

    def dst_part(step):
        return {0: pl.ds(1, 2), 1: pl.ds(0, 1), -1: pl.ds(3, 1)}[step]

    def halo(phase, copy_of, directions=OTHERS):
        def copies(dd, dh):
            slot = (dd + 1) * 3 + dh + 1
            src, dst = copy_of(dd, dh)
            return remote(src, dst, hs.at[phase, slot], hr.at[phase, slot], (d + dd, h + dh))

        def start():
            for dd, dh in directions:
                @pl.when(there(dd, dh))
                def _(dd=dd, dh=dh):
                    copies(dd, dh).start()

        def wait_recv():
            for dd, dh in directions:
                @pl.when(there(-dd, -dh))
                def _(dd=dd, dh=dh):
                    copies(dd, dh).wait_recv()

        def wait_send():
            for dd, dh in directions:
                @pl.when(there(dd, dh))
                def _(dd=dd, dh=dh):
                    copies(dd, dh).wait_send()

        return start, wait_recv, wait_send

    def field_halo(phase, field):
        return halo(
            phase,
            lambda dd, dh: (
                field.at[src_part(dd), src_part(dh)],
                field.at[dst_part(dd), dst_part(dh)],
            ),
        )

    along_h = lambda p: (d, p)
    along_d = lambda p: (p, h)

    def line_h(phase, source, slot):
        return Spread(h, nh, along_h, source, slot, ssem.at[phase], rsem.at[phase])

    def line_d(phase, source, slot):
        return Spread(d, nd, along_d, source, slot, ssem.at[phase], rsem.at[phase])

    sends = []
    rows_out = line_h(0, lambda p: bottom.at[0, pl.ds(first_row(p), 3)], lambda s: brecv.at[s])
    rows_out.start()
    skip_start, skip_recv, skip_send = halo(
        0,
        lambda dd, dh: (
            skip.at[own_part(dd), own_part(dh)],
            joined.at[dst_part(dd), dst_part(dh), :, pl.ds(cu, cu)],
        ),
    )
    skip_start()
    own_rows.wait()
    rows_out.wait_recv()
    for r in range(3):
        row = h - 1 + r
        here = jnp.logical_and(row >= 0, row < nh)
        at = jnp.clip(row - first_row(h), 0, 2)
        pieces = [brecv[c, at].astype(F32) for c in range(nh)]
        line = jnp.concatenate(pieces, axis=1)
        bg[d, r] = jnp.where(here, line, 0.0).astype(BF16)

    near_start, _, near_send = halo(
        1, lambda dd, dh: (bg.at[d, pl.ds(0, 1)], bg.at[d, pl.ds(0, 1)]), [(-1, 0), (1, 0)]
    )
    near_start()
    planes_out = line_d(1, lambda p: bg.at[d, pl.ds(1, 2)], lambda s: bg.at[s, pl.ds(1, 2)])
    planes_out.start()
    weights[0].wait()

    for dd in (-1, 1):
        @pl.when(there(dd, 0))
        def _(dd=dd):
            peer = d + dd
            slot = (-dd + 1) * 3 + 1
            remote(
                bg.at[peer, pl.ds(0, 1)], bg.at[peer, pl.ds(0, 1)], hs.at[1, slot], hr.at[1, slot], (peer, h)
            ).wait_recv()
    planes_out.wait_recv()

    coarse = []
    for s in range(3):
        plane = d - 1 + s
        here = jnp.logical_and(plane >= 0, plane < nd)
        value = bg[jnp.clip(plane, 0, nd - 1)]
        coarse.append(jnp.where(here, value, jnp.zeros_like(value)))
    coarse = jnp.stack(coarse)
    first_of = {0: 1, 1: 1, 2: 0}
    for gd in range(2):
        for gh in range(2):
            total = None
            for kd in ((1,), (0, 2))[gd]:
                for kh in ((1,), (0, 2))[gh]:
                    a, b = first_of[kd], first_of[kh]
                    lhs = coarse[a : a + 2, b : b + 2].reshape(4 * cw, -1)
                    t = kd * 9 + kh * 3
                    rhs = jnp.concatenate([upw[t], upw[t + 1], upw[t + 2]], axis=1)
                    part = dot(lhs, rhs)
                    total = part if total is None else total + part
            even = total[:, cu : 2 * cu]
            odd = total[:, 2 * cu :] + shift_rows(total[:, :cu], -1, cw)
            for i in range(2):
                for j in range(2):
                    at = (i * 2 + j) * cw
                    fd, fh = 2 * i + 1 - gd, 2 * j + 1 - gh
                    up32[fd, fh, pl.ds(0, cw, stride=2), :] = even[at : at + cw]
                    up32[fd, fh, pl.ds(1, cw, stride=2), :] = odd[at : at + cw]
    for fd in range(4):
        for fh in range(4):
            inside = None
            for pos, f, count in ((d, fd, nd), (h, fh, nh)):
                cond = None
                if f == 0:
                    cond = pos > 0
                if f == 3:
                    cond = pos < count - 1
                if cond is not None:
                    inside = cond if inside is None else jnp.logical_and(inside, cond)
            value = up32[fd, fh]
            if inside is not None:
                value = jnp.where(inside, value, 0.0)
            joined[fd, fh, :, 0:cu] = value.astype(BF16)

    own_skip.wait()
    skip_recv()
    weights[1].wait()
    cells = 4 * 2 * cw

    def conv(field, weight):
        chans = field.shape[3]
        lhs = jnp.concatenate(
            [field[a : a + 2, b : b + 2].reshape(cells, chans) for a, b in GRID9], axis=1
        )
        rhs = jnp.concatenate(
            [
                jnp.concatenate([weight[(a * 3 + b) * 3 + c] for c in range(3)], axis=1)
                for a, b in GRID9
            ],
            axis=0,
        )
        y = dot(lhs, rhs)
        n = weight.shape[2]
        return shift_rows(y[:, :n], 1, 2 * cw) + y[:, n : 2 * n] + shift_rows(y[:, 2 * n :], -1, 2 * cw)

    def conv_back(field, weight):
        chans = field.shape[3]
        lhs = jnp.concatenate(
            [field[2 - a : 4 - a, 2 - b : 4 - b].reshape(cells, chans) for a, b in GRID9], axis=1
        )
        rhs = jnp.concatenate(
            [
                jnp.concatenate([weight[(a * 3 + b) * 3 + c] for a, b in GRID9], axis=1)
                for c in range(3)
            ],
            axis=0,
        )
        y = dot(lhs, rhs, NT)
        n = weight.shape[1]
        return shift_rows(y[:, :n], -1, 2 * cw) + y[:, n : 2 * n] + shift_rows(y[:, 2 * n :], 1, 2 * cw)

    first_pre = conv(joined, w1)
    fp[...] = first_pre
    hidden = (first_pre * jax.nn.sigmoid(first_pre)).astype(BF16)
    hid[1:3, 1:3] = hidden.reshape(2, 2, 2 * cw, cu)
    hid_start, hid_recv, hid_send = field_halo(2, hid)
    hid_start()
    hg[d] = hidden
    jg[d] = joined[1:3, 1:3].reshape(cells, 2 * cu)
    hid_out = line_d(2, lambda p: hg.at[d], lambda s: hg.at[s])
    joined_out = line_d(3, lambda p: jg.at[d], lambda s: jg.at[s])
    hid_out.start()

    weights[2].wait()
    weights[3].wait()
    hid_recv()
    second_pre = conv(hid, w2)
    result[...] = (second_pre * jax.nn.sigmoid(second_pre)).astype(BF16).reshape(2, 2, 2 * cw, cu)
    err2 = (cot[...].reshape(cells, cu).astype(F32) * slope(second_pre)).astype(BF16)
    e2[1:3, 1:3] = err2.reshape(2, 2, 2 * cw, cu)
    e2_start, e2_recv, e2_send = field_halo(3, e2)
    e2_start()
    joined_out.start()

    e2_recv()
    err1 = (conv_back(e2, w2) * slope(fp[...])).astype(BF16)
    e1[1:3, 1:3] = err1.reshape(2, 2, 2 * cw, cu)
    e1_start, e1_recv, e1_send = field_halo(4, e1)
    e1_start()

    def flip(field, phase, out, into):
        value = field[1:3].reshape(2 * cells, cu).astype(F32)
        out[...] = value.T
        into[d] = out[pl.ds(pl.multiple_of(d * no, no), no)]
        spread = line_d(
            phase, lambda p: out.at[pl.ds(pl.multiple_of(p * no, no), no)], lambda s: into.at[s]
        )
        spread.start()
        return spread

    e2_out = flip(e2, 4, et2s, et2r)

    e1_recv()
    back = conv_back(e1, w1)
    bu32[...] = back[:, :cu].reshape(2, 2, 2 * cw, cu)
    for i in range(2):
        for j in range(2):
            for par in range(2):
                bu[1 + i, 1 + j, par] = bu32[i, j, pl.ds(par, cw, stride=2), :].astype(BF16)
    bu_start, bu_recv, bu_send = halo(
        5,
        lambda dd, dh: (
            bu.at[pl.ds(2, 1) if dd else pl.ds(1, 2), pl.ds(2, 1) if dh else pl.ds(1, 2)],
            bu.at[pl.ds(0, 1) if dd else pl.ds(1, 2), pl.ds(0, 1) if dh else pl.ds(1, 2)],
        ),
        [(1, 0), (0, 1), (1, 1)],
    )
    bu_start()
    buts[...] = bu[1:3, 1:3].reshape(cells, cu).astype(F32).T
    butr[d] = buts[pl.ds(pl.multiple_of(d * no, no), no)]
    bu_out = line_d(
        5, lambda p: buts.at[pl.ds(pl.multiple_of(p * no, no), no)], lambda s: butr.at[s]
    )
    bu_out.start()
    e1_out = flip(e1, 6, et1s, et1r)
    gskip[...] = back[:, cu:].astype(BF16).reshape(2, 2, 2 * cw, cu)

    def weight_grad(into, gathered, acc):
        a0 = into[:, :, 0 * 128 : 1 * 128].reshape(nd * no, 128)
        b0 = into[:, :, 1 * 128 : 2 * 128].reshape(nd * no, 128)
        a1 = into[:, :, 2 * 128 : 3 * 128].reshape(nd * no, 128)
        b1 = into[:, :, 3 * 128 : 4 * 128].reshape(nd * no, 128)
        lane = lax.broadcasted_iota(jnp.int32, a0.shape, 1)
        zero = jnp.zeros((9 * no, 128), F32)
        for low, high, vt in ((a0, b0, vt0), (a1, b1, vt1)):
            vt[0] = zero
            vt[nd + 1] = zero
            mid = jnp.where(lane < 64, pltpu.roll(low, 64, 1), pltpu.roll(high, 64, 1))
            for kh, rows in enumerate((high, mid, low)):
                for kw in range(3):
                    value = rows if kw == 1 else shift_lanes(rows, kw - 1, 2 * cw)
                    at = (kh * 3 + kw) * no
                    vt[1 : nd + 1, at : at + no, :] = value.reshape(nd, no, 128)
        acc[...] = jnp.zeros_like(acc)

        def step(j, carry):
            lhs = jnp.concatenate(
                [
                    jnp.concatenate([vt1[j + 1], vt0[j + 2]], axis=1),
                    jnp.concatenate([vt0[j + 1], vt1[j + 1]], axis=1),
                    jnp.concatenate([vt1[j], vt0[j + 1]], axis=1),
                ],
                axis=0,
            ).astype(BF16)
            acc[...] += dot(lhs, gathered[j])
            return carry

        lax.fori_loop(0, nd, step, 0)
        return acc[...] * factor

    def flipped(value):
        rows, lanes = value.shape
        tall, wide = round_up(rows, 128), round_up(lanes, 128)
        if tall > rows:
            value = jnp.concatenate([value, jnp.zeros((tall - rows, lanes), F32)], axis=0)
        if wide > lanes:
            value = jnp.concatenate([value, jnp.zeros((tall, wide - lanes), F32)], axis=1)
        return value.T

    def scatter_rows(phase, value, chunk, out, into):
        turned = flipped(value)
        for c in range(nh):
            out[c, 0:chunk, :] = turned[c * chunk : (c + 1) * chunk]
        into[h] = out[h]
        spread = line_h(phase, lambda p: out.at[p], lambda s: into.at[s])
        spread.start()
        return spread

    e2_out.wait_recv()
    hid_out.wait_recv()
    g2_out = scatter_rows(7, weight_grad(et2r, hg, acc2), gsecond.shape[1], gs2, gr2)

    bu_recv()
    around = lambda par: [bu[a, b, par].reshape(cw, cu) for a, b in GRID9]
    lhs = jnp.concatenate(around(0) + around(1), axis=1)
    rhs = jnp.concatenate(
        [upw[(a * 3 + b) * 3 + 1] for a, b in GRID9] + [upw[(a * 3 + b) * 3 + 2] for a, b in GRID9], axis=1
    )
    same = dot(lhs, rhs, NT)
    lhs = jnp.concatenate(around(1), axis=1)
    rhs = jnp.concatenate([upw[(a * 3 + b) * 3] for a, b in GRID9], axis=1)
    block_grad = same + shift_rows(dot(lhs, rhs, NT), 1, cw)
    for c in range(nh):
        cgs[c] = block_grad[:, c * cb : (c + 1) * cb].astype(BF16)
    cgr[h] = cgs[h]
    cg_out = line_h(8, lambda p: cgs.at[p], lambda s: cgr.at[s])
    cg_out.start()

    bu_out.wait_recv()
    per = 128 // cw
    lane = lax.broadcasted_iota(jnp.int32, (no, 128), 1) // cw
    phases = {}
    for pd in range(2):
        for p in range(per):
            groups = []
            for g in range(nd // per):
                total = None
                for s in range(per):
                    piece = butr[g * per + s, :, pd * 128 : (pd + 1) * 128]
                    turn = ((s - p) * cw) % 128
                    piece = pltpu.roll(piece, turn, 1) if turn else piece
                    total = piece if total is None else jnp.where(lane == s, piece, total)
                groups.append(total)
            phases[pd, p // 2, p % 2] = jnp.concatenate(groups, axis=1) if len(groups) > 1 else groups[0]
    wide = lax.broadcasted_iota(jnp.int32, (no, nd * cw), 1)

    def tap_rows(kd, kh, kw):
        pd, sd = PARITY_SHIFT[kd]
        ph, _ = PARITY_SHIFT[kh]
        pw, sw = PARITY_SHIFT[kw]
        value = phases[pd, ph, pw]
        if sw:
            value = shift_lanes(value, 1, cw)
        if sd:
            value = jnp.where(wide < cw, 0.0, pltpu.roll(value, cw, 1))
        return value

    products = {}
    for sh, khs in ((0, (1, 2)), (1, (0,))):
        order = [(kd, kh, kw) for kh in khs for kd in range(3) for kw in range(3)]
        lhs = jnp.concatenate([tap_rows(*k) for k in order], axis=0).astype(BF16)
        rhs = bg[:, 1 + sh].reshape(nd * cw, -1)
        value = dot(lhs, rhs)
        for i, k in enumerate(order):
            products[k] = value[i * no : (i + 1) * no]
    grad_up = jnp.concatenate(
        [products[kd, kh, kw] for kd in range(3) for kh in range(3) for kw in range(3)], axis=0
    )
    gu_out = scatter_rows(9, grad_up * factor, cb, gsu, gru)

    e1_out.wait_recv()
    joined_out.wait_recv()
    g1_out = scatter_rows(10, weight_grad(et1r, jg, acc1), gfirst.shape[1], gs1, gr1)

    def finish(spread, into, out):
        spread.wait_recv()
        total = into[0]
        for s in range(1, nh):
            total = total + into[s]
        rows = out.shape[1]
        for t in range(taps):
            out[t] = total[:rows, t * no : (t + 1) * no]

    finish(g2_out, gr2, gsecond)
    cg_out.wait_recv()
    cgrad[...] = cgr[...]
    finish(gu_out, gru, gup)
    finish(g1_out, gr1, gfirst)

    for spread in (
        rows_out, planes_out, hid_out, joined_out, e2_out, e1_out, bu_out, g2_out, cg_out, gu_out, g1_out
    ):
        spread.wait_send()
    for wait in (skip_send, near_send, hid_send, e2_send, e1_send, bu_send):
        wait()


def per_device(nd, nh, bottom, skip, upconv_kernel, w_first, w_second, cotangent):
    cb, cw = bottom.shape[3], bottom.shape[2]
    cin, cu = upconv_kernel.shape[3:]
    fw = skip.shape[2]
    cj = w_first.shape[3]
    no = cu // nd
    rows = skip.shape[:2]
    factor = 1.0 / math.sqrt(rows[0] * nd * rows[1] * nh * fw)
    taps = round_up(27 * no, 128)
    ncj, nch = cj // nh, cu // nh
    v = pltpu.VMEM
    upw = upconv_kernel.reshape(27, cin, cu)
    w1 = w_first.reshape(27, cj, cu)
    w2 = w_second.reshape(27, cu, cu)
    cells = rows[0] * rows[1] * fw
    line = max(nd, nh)
    scratch = [
        v(upw.shape, BF16), v(w1.shape, BF16), v(w2.shape, BF16), v(cotangent.shape, BF16),
        v((nh, 3, cw, cb), BF16),
        v((nd, 3, cw, cin), BF16),
        v((4, 4, fw, cu), F32),
        v((4, 4, fw, cj), BF16),
        v((nd, cells, cj), BF16),
        v((cells, cu), F32),
        v((4, 4, fw, cu), BF16),
        v((nd, cells, cu), BF16),
        v((4, 4, fw, cu), BF16),
        v((4, 4, fw, cu), BF16),
        v((cu, 2 * cells), F32), v((nd, no, 2 * cells), F32),
        v((cu, 2 * cells), F32), v((nd, no, 2 * cells), F32),
        v((2, 2, fw, cu), F32),
        v((3, 3, 2, cw, cu), BF16),
        v((cu, cells), F32), v((nd, no, cells), F32),
        v((nh, cw, cb), BF16), v((nh, cw, cb), BF16),
        v((nd + 2, 9 * no, 128), F32), v((nd + 2, 9 * no, 128), F32),
        v((27 * no, cj), F32), v((27 * no, cu), F32),
        v((nh, round_up(nch, 8), taps), F32), v((nh, round_up(nch, 8), taps), F32),
        v((nh, round_up(ncj, 8), taps), F32), v((nh, round_up(ncj, 8), taps), F32),
        v((nh, round_up(cb, 8), taps), F32), v((nh, round_up(cb, 8), taps), F32),
        pltpu.SemaphoreType.DMA((11, line)), pltpu.SemaphoreType.DMA((11, line)),
        pltpu.SemaphoreType.DMA((6, 9)), pltpu.SemaphoreType.DMA((6, 9)),
        pltpu.SemaphoreType.DMA((6,)),
    ]
    outs = [
        jax.ShapeDtypeStruct(skip.shape, BF16),
        jax.ShapeDtypeStruct((nh, cw, cb), BF16),
        jax.ShapeDtypeStruct(skip.shape, BF16),
        jax.ShapeDtypeStruct((27, cb, no), F32),
        jax.ShapeDtypeStruct((27, ncj, no), F32),
        jax.ShapeDtypeStruct((27, nch, no), F32),
    ]
    result, cgrad, gskip, gup, gfirst, gsecond = pl.pallas_call(
        functools.partial(body, nd, nh, factor),
        out_shape=outs,
        in_specs=[pl.BlockSpec(memory_space=pl.ANY)] * 6,
        out_specs=[pl.BlockSpec(memory_space=pltpu.VMEM)] * 6,
        scratch_shapes=scratch,
        compiler_params=pltpu.CompilerParams(
            collective_id=0, has_side_effects=True, vmem_limit_bytes=56 * 1024 * 1024
        ),
        name="decoder",
    )(bottom, skip, upw, w1, w2, cotangent)
    return (
        result,
        cgrad[None],
        gskip,
        gup.reshape(3, 3, 3, cb, no),
        gfirst.reshape(3, 3, 3, ncj, no),
        gsecond.reshape(3, 3, 3, nch, no),
    )


def solution(mesh):
    return jax.shard_map(
        functools.partial(per_device, mesh.shape["depth"], mesh.shape["height"]),
        mesh=mesh,
        in_specs=(
            P("depth", None, None, "height"),
            P("depth", "height", None, None),
            P(),
            P(),
            P(),
            P("depth", "height", None, None),
        ),
        out_specs=(
            P("depth", "height", None, None),
            P("depth", None, None, "height"),
            P("depth", "height", None, None),
            P(None, None, None, "height", "depth"),
            P(None, None, None, "height", "depth"),
            P(None, None, None, "height", "depth"),
        ),
        check_vma=False,
    )
```

time: 1120 us -> 130 us (0.12)
  waiting for transfers between devices: 823 us -> 0 us
  Pallas kernels: 0 us -> 118 us
  starting transfers between devices: 73.7 us -> 0 us
  local copies, waits for them, and re-layouts: 79.2 us -> 11.5 us
  matrix products: 66 us -> 0 us
  blocking collectives: 38 us -> 0 us
  between operations: 17.4 us -> 0.64 us
    unnamed x9 -> x0, waiting for transfers between devices: 748 us -> none
    pallas_call x0 -> x1, Pallas kernels: none -> 118 us  [per_device(): pl.pallas_call(functools.partial(body, nd, nh, factor), out_shape=outs, i...]
    ppermute x20 -> x0, starting transfers between devices: 73.2 us -> none  [the longest x8 43.2 us: extended(): before = lax.ppermute(last, axis, up)]
    dot_general x243 -> x0, matrix products: 66 us -> none  [the longest x54 29.2 us: conv_weight(): lax.dot_general(sliced.reshape(-1, padded.shape[3]), flat_err, (((0,), (0...]
    reduce_scatter x1 -> x0, waiting for transfers between devices: 59.6 us -> none  [per_device(): lax.psum_scatter(g_first_local, 'depth', scatter_dimension=4, tiled=True)]
    all_to_all x2 -> x0, blocking collectives: 38 us -> none  [the longest x1 20.3 us: per_device(): lax.all_to_all(bottom, 'height', split_axis=1, concat_axis=3, tiled=True)]
    unnamed x117 -> x7, local copies, waits for them, and re-layouts: 37.1 us -> 11.5 us
    slice x48 -> x0, local copies, waits for them, and re-layouts: 23.2 us -> none  [the longest x27 20.5 us: reduce_resolution(): widened_volume[tap_d:tap_d + 2 * coarse[0]:2, tap_h:tap_h + 2 * coarse[1]...]
  transfers between devices with their start and end apart: 25 -> 0, of which waited for: 15 -> 0; matrix products, arithmetic and copies ran while one was open for 7% -> 0% of each run, Pallas kernels for 0% -> 0%
where the time goes in v1:
time: 130 us
  Pallas kernels  118 us (91%)
  local copies, waits for them, and re-layouts  11.5 us (9%)
    pallas_call x1, Pallas kernels, per_device(): pl.pallas_call(functools.partial(body, nd, nh, factor), out_shape=outs, i...  118 us
    unnamed x7, local copies, waits for them, and re-layouts  11.5 us

profile of v1, /device:TPU:1, one launch (start us, length us, event | category | flops | bytes accessed | tf_op | source)
XLA Modules:
  0.0 129.8 jit_solution(12046001726054819033)
XLA Ops:
  0.6 1.7 %copy.12.bottom = bf16[1,16,32,20]{3,2,1,0:T(8,128)(2,1)} copy(bf16[1,16,32,20]{2,1,3,0:T(8,128)(2,1)} %param.6) | data formatting | bytes 40960 | tf_op args[0]
  2.3 117.7 %decoder.1 = (bf16[2,2,64,128]{3,2,1,0:T(8,128)(2,1)}, bf16[16,32,20]{2,1,0:T(8,128)(2,1)}, bf16[2,2,64,128]{3,2,1,0:T(8,128)(2,1)}, f32[27,20,8]{2,1,0:T(8,128)...) custom-call(bf16[1,16,32,20]{3,2,1,0:T(8,128)(2,1)} %copy.12.bottom, bf16[2,2,64,128]{3,2,1,0:T(8,128)(2,1)} %skip.1, ...), custom_call_target="tpu_custom_call" | custom-call | tf_op jit(solution)/shard_map/decoder/pallas_call | solution.py:579
  120.1 1.7 %copy.13 = bf16[1,16,32,20]{2,1,3,0:T(8,128)(2,1)} copy(bf16[1,16,32,20]{3,2,1,0:T(8,128)(2,1)} %bitcast.12) | data formatting | bytes 40960
  121.8 1.8 %copy.14 = f32[3,3,3,20,8]{3,4,2,1,0:T(8,128)} copy(f32[3,3,3,20,8]{4,3,2,1,0:T(8,128)} %bitcast.10) | data formatting | bytes 34560
  123.6 1.7 %copy.15 = f32[3,3,3,16,8]{3,4,2,1,0:T(8,128)} copy(f32[3,3,3,16,8]{4,3,2,1,0:T(8,128)} %bitcast.11) | data formatting | bytes 27648
  125.3 1.5 %copy.19 = bf16[2,2,64,128]{3,2,1,0:T(8,128)(2,1)} copy(bf16[2,2,64,128]{3,2,1,0:T(8,128)(2,1)} %get-tuple-element.30) | data formatting | bytes 131072
  126.8 1.5 %copy.20 = bf16[2,2,64,128]{3,2,1,0:T(8,128)(2,1)} copy(bf16[2,2,64,128]{3,2,1,0:T(8,128)(2,1)} %get-tuple-element.32) | data formatting | bytes 131072
  128.3 1.5 %copy.21 = f32[3,3,3,8,8]{4,3,2,1,0:T(8,128)} copy(f32[3,3,3,8,8]{4,3,2,1,0:T(8,128)} %bitcast.13) | data formatting | bytes 13824

commit v2 on v1

v2 whole, which is shorter than its diff:
```python
import functools
import math

import jax
import jax.numpy as jnp
from jax import lax
from jax.experimental import pallas as pl
from jax.experimental.pallas import tpu as pltpu
from jax.sharding import PartitionSpec as P

MESH = pl.DeviceIdType.MESH
F32 = jnp.float32
BF16 = jnp.bfloat16
GRID9 = [(a, b) for a in range(3) for b in range(3)]
OTHERS = [(a, b) for a in (-1, 0, 1) for b in (-1, 0, 1) if (a, b) != (0, 0)]
NT = (((1,), (1,)), ((), ()))
PARITY_SHIFT = {0: (1, 1), 1: (0, 0), 2: (1, 0)}


def round_up(value, unit):
    return -(-value // unit) * unit


def remote(src, dst, send, recv, target):
    return pltpu.make_async_remote_copy(
        src_ref=src, dst_ref=dst, send_sem=send, recv_sem=recv, device_id=target, device_id_type=MESH
    )


class Spread:
    def __init__(self, log, me, count, target, source, slot, send, recv, steps=None):
        self.me, self.count, self.target = me, count, target
        self.source, self.slot, self.send, self.recv = source, slot, send, recv
        self.steps = steps or (1, count)
        self.arrived, self.log = False, log

    def each(self, act):
        def step(j, carry):
            act(j)
            return carry

        lax.fori_loop(*self.steps, step, 0)

    def outgoing(self, j):
        peer = lax.rem(self.me + j, self.count)
        return remote(
            self.source(peer), self.slot(self.me), self.send.at[peer], self.recv.at[self.me], self.target(peer)
        )

    def incoming(self, j):
        peer = lax.rem(self.me + self.count - j, self.count)
        return remote(
            self.source(peer), self.slot(peer), self.send.at[peer], self.recv.at[peer], self.target(peer)
        )

    def start(self):
        self.log.append(self)
        self.each(lambda j: self.outgoing(j).start())

    def wait_recv(self):
        self.arrived = True
        self.each(lambda j: self.incoming(j).wait_recv())

    def wait_send(self):
        self.each(lambda j: self.outgoing(j).wait_send())


class Halo:
    def __init__(self, log, there, copy, directions):
        self.there, self.copy, self.directions = there, copy, directions
        self.arrived, self.log = False, log

    def each(self, sign, act):
        for dd, dh in self.directions:
            @pl.when(self.there(sign * dd, sign * dh))
            def _(dd=dd, dh=dh):
                act(self.copy(dd, dh))

    def start(self):
        self.log.append(self)
        self.each(1, lambda copy: copy.start())

    def wait_recv(self):
        self.arrived = True
        self.each(-1, lambda copy: copy.wait_recv())

    def wait_send(self):
        self.each(1, lambda copy: copy.wait_send())


def shift_rows(value, by, period):
    rows = value.shape[0]
    row = lax.broadcasted_iota(jnp.int32, value.shape, 0) % period
    edge = 0 if by > 0 else period - 1
    return jnp.where(row == edge, 0.0, pltpu.roll(value, by % rows, 0))


def shift_lanes(value, by, period):
    lanes = value.shape[1]
    lane = lax.broadcasted_iota(jnp.int32, value.shape, 1) % period
    edge = 0 if by > 0 else period - 1
    return jnp.where(lane == edge, 0.0, pltpu.roll(value, by % lanes, 1))


def slope(values):
    sig = jax.nn.sigmoid(values)
    return sig * (1.0 + values * (1.0 - sig))


def dot(a, b, dims=(((1,), (0,)), ((), ()))):
    return lax.dot_general(a, b, dims, preferred_element_type=F32)


def body(
    nd, nh, factor,
    bottom, skip, upw_hbm, w1_hbm, w2_hbm, cot_hbm,
    result, gskip, cgrows, sumup, sumfirst, sumsecond,
    upw, w1, w2, cot, bott, bsend, brecv, near, bg, up32, joined, jg, fp, hid, hg, e2, e1, et2s, et2r, et1s, et1r,
    bu32, bu, buts, butr, cgs, cgr, acc1, acc2, px2, pr2, px1, pr1, pxu, pru, gs2, gr2, gs1, gr1, gsu, gru,
    ssem, rsem, hs, hr, loc,
):
    d = lax.axis_index("depth")
    h = lax.axis_index("height")
    pair, core = d // 2, lax.rem(d, 2)
    partner = d + 1 - 2 * core
    npair = nd // 2
    cb, rows_all, cw = bottom.shape
    cu = upw.shape[2]
    cin = upw.shape[1]
    no = cu // nd
    both = 2 * no

    weights = [
        pltpu.make_async_copy(upw_hbm, upw, loc.at[0]),
        pltpu.make_async_copy(w1_hbm, w1, loc.at[1]),
        pltpu.make_async_copy(w2_hbm, w2, loc.at[2]),
        pltpu.make_async_copy(cot_hbm, cot, loc.at[3]),
    ]
    own_skip = pltpu.make_async_copy(skip, joined.at[pl.ds(1, 2), pl.ds(1, 2), :, pl.ds(cu, cu)], loc.at[4])

    joined[...] = jnp.zeros_like(joined)
    hid[...] = jnp.zeros_like(hid)
    e2[...] = jnp.zeros_like(e2)
    e1[...] = jnp.zeros_like(e1)
    bu[...] = jnp.zeros_like(bu)

    own_skip.start()
    for copy in weights:
        copy.start()

    barrier = pltpu.get_barrier_semaphore()

    def greet_line(count, target):
        def step(j, carry):
            pl.semaphore_signal(barrier, inc=1, device_id=target(j), device_id_type=MESH)
            return carry

        lax.fori_loop(1, count, step, 0)

    greet_line(nh, lambda j: (d, lax.rem(h + j, nh)))
    greet_line(npair, lambda j: (2 * lax.rem(pair + j, npair) + core, h))

    def there(dd, dh):
        ok = None
        for pos, step, count in ((d, dd, nd), (h, dh, nh)):
            if step:
                cond = pos > 0 if step < 0 else pos < count - 1
                ok = cond if ok is None else jnp.logical_and(ok, cond)
        return ok

    for dd in (-1, 1):
        for dh in (-1, 0, 1):
            target = (lax.rem(d + dd + nd, nd), lax.rem(h + dh + nh, nh))
            pl.semaphore_signal(barrier, inc=1, device_id=target, device_id_type=MESH)

    bott[...] = bottom[...].astype(F32).reshape(cb * rows_all, cw)
    lines = [bott[pl.ds(r, cb, stride=rows_all), :] for r in range(rows_all)]
    blank = jnp.zeros((cb, cw), F32)
    rest = jnp.zeros((cb, 128 - 3 * cw), F32)
    pad = jnp.zeros((bsend.shape[1] - cb, 128), F32)
    for p in range(nh):
        before = lines[p - 1] if p > 0 else blank
        after = lines[p + 1] if p < nh - 1 else blank
        window = jnp.concatenate([before, lines[p], after, rest], axis=1)
        bsend[p] = jnp.concatenate([window, pad], axis=0).astype(BF16)
    brecv[h] = bsend[h]
    pl.semaphore_wait(barrier, nh + npair + 4)

    def src_part(step):
        return {0: pl.ds(1, 2), 1: pl.ds(2, 1), -1: pl.ds(1, 1)}[step]

    def own_part(step):
        return {0: pl.ds(0, 2), 1: pl.ds(1, 1), -1: pl.ds(0, 1)}[step]

    def dst_part(step):
        return {0: pl.ds(1, 2), 1: pl.ds(0, 1), -1: pl.ds(3, 1)}[step]

    log = []

    def halo(phase, copy_of, directions=OTHERS):
        def copy(dd, dh):
            slot = (dd + 1) * 3 + dh + 1
            src, dst = copy_of(dd, dh)
            return remote(src, dst, hs.at[phase, slot], hr.at[phase, slot], (d + dd, h + dh))

        return Halo(log, there, copy, directions)

    def field_halo(phase, field):
        return halo(
            phase,
            lambda dd, dh: (
                field.at[src_part(dd), src_part(dh)],
                field.at[dst_part(dd), dst_part(dh)],
            ),
        )

    def line_h(phase, source, slot):
        return Spread(log, h, nh, lambda p: (d, p), source, slot, ssem.at[phase], rsem.at[phase])

    def line_d(phase, source, slot, steps):
        return Spread(log, d, nd, lambda p: (p, h), source, slot, ssem.at[phase], rsem.at[phase], steps)

    def line_p(phase, source, slot):
        return Spread(
            log, pair, npair, lambda p: (2 * p + core, h), source, slot, ssem.at[phase], rsem.at[phase]
        )

    rows_out = line_h(0, lambda p: bsend.at[p], lambda s: brecv.at[s])
    rows_out.start()
    skip_halo = halo(
        0,
        lambda dd, dh: (
            skip.at[own_part(dd), own_part(dh)],
            joined.at[dst_part(dd), dst_part(dh), :, pl.ds(cu, cu)],
        ),
    )
    skip_halo.start()
    rows_out.wait_recv()
    stack = [brecv[c].astype(F32)[:cb] for c in range(nh)]
    wide = near.shape[3]
    if wide > cin:
        stack.append(jnp.zeros((wide - cin, 128), F32))
    near[1] = jnp.concatenate(stack, axis=0).T[: 3 * cw].reshape(3, cw, wide).astype(BF16)

    plane_next = line_d(1, lambda p: near.at[1], lambda s: near.at[0], (1, 2))
    plane_prev = line_d(2, lambda p: near.at[1], lambda s: near.at[2], (nd - 1, nd))
    plane_next.start()
    plane_prev.start()
    weights[0].wait()
    plane_next.wait_recv()
    plane_prev.wait_recv()

    coarse = []
    for s in range(3):
        plane = d - 1 + s
        here = jnp.logical_and(plane >= 0, plane < nd)
        value = near[s, :, :, 0:cin]
        coarse.append(jnp.where(here, value, jnp.zeros_like(value)))
    coarse = jnp.stack(coarse)
    bg[pair] = jnp.stack([near[1, 1:3], jnp.where(d < nd - 1, near[2, 1:3], jnp.zeros_like(near[2, 1:3]))])
    first_of = {0: 1, 1: 1, 2: 0}
    for gd in range(2):
        for gh in range(2):
            total = None
            for kd in ((1,), (0, 2))[gd]:
                for kh in ((1,), (0, 2))[gh]:
                    a, b = first_of[kd], first_of[kh]
                    lhs = coarse[a : a + 2, b : b + 2].reshape(4 * cw, -1)
                    t = kd * 9 + kh * 3
                    rhs = jnp.concatenate([upw[t], upw[t + 1], upw[t + 2]], axis=1)
                    part = dot(lhs, rhs)
                    total = part if total is None else total + part
            even = total[:, cu : 2 * cu]
            odd = total[:, 2 * cu :] + shift_rows(total[:, :cu], -1, cw)
            for i in range(2):
                for j in range(2):
                    at = (i * 2 + j) * cw
                    fd, fh = 2 * i + 1 - gd, 2 * j + 1 - gh
                    up32[fd, fh, pl.ds(0, cw, stride=2), :] = even[at : at + cw]
                    up32[fd, fh, pl.ds(1, cw, stride=2), :] = odd[at : at + cw]
    for fd in range(4):
        for fh in range(4):
            inside = None
            for pos, f, count in ((d, fd, nd), (h, fh, nh)):
                cond = None
                if f == 0:
                    cond = pos > 0
                if f == 3:
                    cond = pos < count - 1
                if cond is not None:
                    inside = cond if inside is None else jnp.logical_and(inside, cond)
            value = up32[fd, fh]
            if inside is not None:
                value = jnp.where(inside, value, 0.0)
            joined[fd, fh, :, 0:cu] = value.astype(BF16)

    own_skip.wait()
    skip_halo.wait_recv()
    weights[1].wait()
    cells = 4 * 2 * cw

    def conv(field, weight):
        chans = field.shape[3]
        lhs = jnp.concatenate(
            [field[a : a + 2, b : b + 2].reshape(cells, chans) for a, b in GRID9], axis=1
        )
        rhs = jnp.concatenate(
            [
                jnp.concatenate([weight[(a * 3 + b) * 3 + c] for c in range(3)], axis=1)
                for a, b in GRID9
            ],
            axis=0,
        )
        y = dot(lhs, rhs)
        n = weight.shape[2]
        return shift_rows(y[:, :n], 1, 2 * cw) + y[:, n : 2 * n] + shift_rows(y[:, 2 * n :], -1, 2 * cw)

    def conv_back(field, weight):
        chans = field.shape[3]
        lhs = jnp.concatenate(
            [field[2 - a : 4 - a, 2 - b : 4 - b].reshape(cells, chans) for a, b in GRID9], axis=1
        )
        rhs = jnp.concatenate(
            [
                jnp.concatenate([weight[(a * 3 + b) * 3 + c] for a, b in GRID9], axis=1)
                for c in range(3)
            ],
            axis=0,
        )
        y = dot(lhs, rhs, NT)
        n = weight.shape[1]
        return shift_rows(y[:, :n], -1, 2 * cw) + y[:, n : 2 * n] + shift_rows(y[:, 2 * n :], 1, 2 * cw)

    first_pre = conv(joined, w1)
    fp[...] = first_pre
    hidden = (first_pre * jax.nn.sigmoid(first_pre)).astype(BF16)
    hid[1:3, 1:3] = hidden.reshape(2, 2, 2 * cw, cu)
    hid_halo = field_halo(2, hid)
    hid_halo.start()
    hg[pair] = hidden
    jg[pair] = joined[1:3, 1:3].reshape(cells, 2 * cu)
    joined_out = line_p(4, lambda p: jg.at[pair], lambda s: jg.at[s])
    joined_out.start()

    weights[2].wait()
    weights[3].wait()
    hid_halo.wait_recv()
    second_pre = conv(hid, w2)
    result[...] = (second_pre * jax.nn.sigmoid(second_pre)).astype(BF16).reshape(2, 2, 2 * cw, cu)
    err2 = (cot[...].reshape(cells, cu).astype(F32) * slope(second_pre)).astype(BF16)
    e2[1:3, 1:3] = err2.reshape(2, 2, 2 * cw, cu)
    e2_halo = field_halo(3, e2)
    e2_halo.start()
    hid_out = line_p(3, lambda p: hg.at[pair], lambda s: hg.at[s])
    hid_out.start()

    e2_halo.wait_recv()
    err1 = (conv_back(e2, w2) * slope(fp[...])).astype(BF16)
    e1[1:3, 1:3] = err1.reshape(2, 2, 2 * cw, cu)
    e1_halo = field_halo(4, e1)
    e1_halo.start()

    def part_of(p):
        return pl.ds(pl.multiple_of(p * both, both), both)

    def flip(value, phase, out, into):
        out[...] = value.astype(F32).T.astype(BF16)
        into[pair] = out[part_of(pair)]
        spread = line_p(phase, lambda p: out.at[part_of(p)], lambda s: into.at[s])
        spread.start()
        return spread

    e2_out = flip(e2[...].reshape(4 * cells, cu), 5, et2s, et2r)
    planes_out = line_p(6, lambda p: bg.at[pair], lambda s: bg.at[s])
    planes_out.start()

    e1_halo.wait_recv()
    back = conv_back(e1, w1)
    bu32[...] = back[:, :cu].reshape(2, 2, 2 * cw, cu)
    for i in range(2):
        for j in range(2):
            for par in range(2):
                bu[1 + i, 1 + j, par] = bu32[i, j, pl.ds(par, cw, stride=2), :].astype(BF16)
    bu_halo = halo(
        5,
        lambda dd, dh: (
            bu.at[pl.ds(2, 1) if dd else pl.ds(1, 2), pl.ds(2, 1) if dh else pl.ds(1, 2)],
            bu.at[pl.ds(0, 1) if dd else pl.ds(1, 2), pl.ds(0, 1) if dh else pl.ds(1, 2)],
        ),
        [(1, 0), (0, 1), (1, 1)],
    )
    bu_halo.start()
    bu_out = flip(bu[1:3, 1:3].reshape(cells, cu), 7, buts, butr)
    e1_out = flip(e1[...].reshape(4 * cells, cu), 8, et1s, et1r)
    gskip[...] = back[:, cu:].astype(BF16).reshape(2, 2, 2 * cw, cu)

    def weight_grad(into, gathered, acc):
        acc[...] = jnp.zeros_like(acc)
        half = 2 * cw
        per_plane = 4 * half
        lane = lax.broadcasted_iota(jnp.int32, (both, 128), 1)

        def step(j, carry):
            shifted = []
            for plane in range(4):
                at = plane * per_plane
                low = into[j, :, at : at + 128].astype(F32)
                high = into[j, :, at + 128 : at + 256].astype(F32)
                mid = jnp.where(lane < half, pltpu.roll(low, half, 1), pltpu.roll(high, half, 1))
                shifted.append(
                    [
                        rows if kw == 1 else shift_lanes(rows, kw - 1, half)
                        for rows in (high, mid, low)
                        for kw in range(3)
                    ]
                )
            lhs = []
            for c in range(2):
                for kd in range(3):
                    for k in range(9):
                        pieces = [shifted[2 - kd + q][k][c * no : (c + 1) * no] for q in range(2)]
                        lhs.append(jnp.concatenate(pieces, axis=1))
            acc[...] += dot(jnp.concatenate(lhs, axis=0).astype(BF16), gathered[j])
            return carry

        lax.fori_loop(0, npair, step, 0)
        return acc[...]

    def swap(phase, value, out, into):
        half = 27 * no
        halves = [value[:half], value[half:]]
        mine = jnp.where(core == 0, halves[0], halves[1])
        out[...] = jnp.where(core == 0, halves[1], halves[0])
        copy = line_d(phase, lambda p: out, lambda s: into, (1, 2))
        copy.target = lambda p: (partner, h)
        copy.outgoing = copy.incoming = lambda j: remote(
            out, into, ssem.at[phase, 0], rsem.at[phase, 0], (partner, h)
        )
        copy.start()
        return copy, mine

    def flipped(value):
        rows, lanes = value.shape
        tall, wide = round_up(rows, 128), round_up(lanes, 128)
        if tall > rows:
            value = jnp.concatenate([value, jnp.zeros((tall - rows, lanes), F32)], axis=0)
        if wide > lanes:
            value = jnp.concatenate([value, jnp.zeros((tall, wide - lanes), F32)], axis=1)
        return value.T

    def scatter_rows(phase, swapped, arriving, chunk, out, into):
        copy, mine = swapped
        copy.wait_recv()
        turned = flipped((mine + arriving[...]) * factor)
        fill = out.shape[1] - chunk
        for c in range(nh):
            piece = turned[c * chunk : (c + 1) * chunk]
            if fill:
                piece = jnp.concatenate([piece, jnp.zeros((fill, piece.shape[1]), F32)], axis=0)
            out[c] = piece.astype(out.dtype)
        into[h] = out[h]
        spread = line_h(phase, lambda p: out.at[p], lambda s: into.at[s])
        spread.start()
        return spread

    e2_out.wait_recv()
    hid_out.wait_recv()
    swap2 = swap(9, weight_grad(et2r, hg, acc2), px2, pr2)

    bu_halo.wait_recv()
    around = lambda par: [bu[a, b, par].reshape(cw, cu) for a, b in GRID9]
    lhs = jnp.concatenate(around(0) + around(1), axis=1)
    rhs = jnp.concatenate(
        [upw[(a * 3 + b) * 3 + 1] for a, b in GRID9] + [upw[(a * 3 + b) * 3 + 2] for a, b in GRID9], axis=1
    )
    same = dot(lhs, rhs, NT)
    lhs = jnp.concatenate(around(1), axis=1)
    rhs = jnp.concatenate([upw[(a * 3 + b) * 3] for a, b in GRID9], axis=1)
    block_grad = flipped(same + shift_rows(dot(lhs, rhs, NT), 1, cw))
    for c in range(nh):
        cgs[c, 0:cb] = block_grad[c * cb : (c + 1) * cb]
    cgr[h] = cgs[h]
    cg_out = line_h(10, lambda p: cgs.at[p], lambda s: cgr.at[s])
    cg_out.start()
    g2_out = scatter_rows(11, swap2, pr2, cu // nh, gs2, gr2)

    bu_out.wait_recv()
    per = 128 // cw
    span = npair * cw
    group = min(per, npair)
    lane = lax.broadcasted_iota(jnp.int32, (both, 128), 1) // cw
    phases = {}
    for pd in range(2):
        for p in range(per):
            groups = []
            for g in range(npair // group):
                total = None
                for s in range(group):
                    piece = butr[g * group + s, :, pd * 128 : (pd + 1) * 128].astype(F32)
                    turn = ((s - p) * cw) % 128
                    piece = pltpu.roll(piece, turn, 1) if turn else piece
                    total = piece if total is None else jnp.where(lane == s, piece, total)
                groups.append(total)
            value = jnp.concatenate(groups, axis=1) if len(groups) > 1 else groups[0]
            phases[pd, p // 2, p % 2] = value[:, :span]

    def tap_rows(kd, kh, kw):
        pw, sw = PARITY_SHIFT[kw]
        value = phases[PARITY_SHIFT[kd][0], PARITY_SHIFT[kh][0], pw]
        return shift_lanes(value, 1, cw) if sw else value

    planes_out.wait_recv()
    products = {}
    for sd, kds in ((0, (1, 2)), (1, (0,))):
        for sh, khs in ((0, (1, 2)), (1, (0,))):
            order = [(kd, kh, kw) for kd in kds for kh in khs for kw in range(3)]
            lhs = jnp.concatenate([tap_rows(*k) for k in order], axis=0).astype(BF16)
            rhs = bg[:, sd, sh].reshape(span, -1)
            value = dot(lhs, rhs)
            for i, k in enumerate(order):
                for c in range(2):
                    at = (i * 2 + c) * no
                    products[(c,) + k] = value[at : at + no]
    grad_up = jnp.concatenate(
        [products[c, a, b, e] for c in range(2) for a, b in GRID9 for e in range(3)], axis=0
    )
    swapu = swap(12, grad_up, pxu, pru)

    e1_out.wait_recv()
    joined_out.wait_recv()
    swap1 = swap(13, weight_grad(et1r, jg, acc1), px1, pr1)
    gu_out = scatter_rows(14, swapu, pru, cb, gsu, gru)
    g1_out = scatter_rows(15, swap1, pr1, 2 * cu // nh, gs1, gr1)

    def finish(spread, into, out):
        spread.wait_recv()
        total = into[0].astype(F32)
        for s in range(1, nh):
            total = total + into[s].astype(F32)
        out[...] = total[: out.shape[0]]

    finish(g2_out, gr2, sumsecond)
    cg_out.wait_recv()
    cgrows[...] = cgr[...]
    finish(gu_out, gru, sumup)
    finish(g1_out, gr1, sumfirst)

    for part in log:
        if not part.arrived:
            part.wait_recv()
        part.wait_send()


def closing(nh, result, gskip, cgrows, sumup, sumfirst, sumsecond, out0, out1, out2, out3, out4, out5, sems):
    whole = [pltpu.make_async_copy(result, out0, sems.at[0]), pltpu.make_async_copy(gskip, out2, sems.at[1])]
    for copy in whole:
        copy.start()
    cb = out1.shape[0]
    tall = cgrows.shape[0] // nh
    for c in range(cb):
        out1[c] = cgrows[pl.ds(c, nh, stride=tall), 0 : out1.shape[2]].astype(BF16)
    no = out3.shape[1]
    for total, out in ((sumup, out3), (sumfirst, out4)):
        n = out.shape[2]
        turned = total[...]
        if turned.shape[0] < 128:
            fill = jnp.zeros((128 - turned.shape[0], turned.shape[1]), F32)
            turned = jnp.concatenate([turned, fill], axis=0)
        out[...] = turned.T[: 27 * no, :n].reshape(27, no, n)
    total = sumsecond[...]
    for t in range(27):
        out5[t] = total[: out5.shape[1], t * no : (t + 1) * no]
    for copy in whole:
        copy.wait()


def per_device(nd, nh, bottom, skip, upconv_kernel, w_first, w_second, cotangent):
    cb, cw = bottom.shape[3], bottom.shape[2]
    cin, cu = upconv_kernel.shape[3:]
    fw = skip.shape[2]
    cj = w_first.shape[3]
    no = cu // nd
    both, npair = 2 * no, nd // 2
    rows = skip.shape[:2]
    factor = 1.0 / math.sqrt(rows[0] * nd * rows[1] * nh * fw)
    taps = round_up(27 * no, 128)
    ncj, nch = cj // nh, cu // nh
    v = pltpu.VMEM
    upw = upconv_kernel.reshape(27, cin, cu)
    w1 = w_first.reshape(27, cj, cu)
    w2 = w_second.reshape(27, cu, cu)
    cells = rows[0] * rows[1] * fw
    line = max(nd, nh)
    wide = round_up(cin, 128)
    part = 27 * no
    scratch = [
        v(upw.shape, BF16), v(w1.shape, BF16), v(w2.shape, BF16), v(cotangent.shape, BF16),
        v((cb * nh, cw), F32),
        v((nh, round_up(cb, 16), 128), BF16), v((nh, round_up(cb, 16), 128), BF16),
        v((3, 3, cw, wide), BF16),
        v((npair, 2, 2, cw, wide), BF16),
        v((4, 4, fw, cu), F32),
        v((4, 4, fw, cj), BF16),
        v((npair, cells, cj), BF16),
        v((cells, cu), F32),
        v((4, 4, fw, cu), BF16),
        v((npair, cells, cu), BF16),
        v((4, 4, fw, cu), BF16),
        v((4, 4, fw, cu), BF16),
        v((cu, 4 * cells), BF16), v((npair, both, 4 * cells), BF16),
        v((cu, 4 * cells), BF16), v((npair, both, 4 * cells), BF16),
        v((2, 2, fw, cu), F32),
        v((3, 3, 2, cw, cu), BF16),
        v((cu, cells), BF16), v((npair, both, cells), BF16),
        v((nh, round_up(cb, 8), 128), F32), v((nh, round_up(cb, 8), 128), F32),
        v((2 * part, cj), F32), v((2 * part, cu), F32),
        v((part, cu), F32), v((part, cu), F32),
        v((part, cj), F32), v((part, cj), F32),
        v((part, wide), F32), v((part, wide), F32),
        v((nh, round_up(nch, 8), taps), F32), v((nh, round_up(nch, 8), taps), F32),
        v((nh, round_up(ncj, 16), taps), BF16), v((nh, round_up(ncj, 16), taps), BF16),
        v((nh, round_up(cb, 16), taps), BF16), v((nh, round_up(cb, 16), taps), BF16),
        pltpu.SemaphoreType.DMA((16, line)), pltpu.SemaphoreType.DMA((16, line)),
        pltpu.SemaphoreType.DMA((6, 9)), pltpu.SemaphoreType.DMA((6, 9)),
        pltpu.SemaphoreType.DMA((6,)),
    ]
    tall = round_up(cb, 8)
    shape = jax.ShapeDtypeStruct
    left = pl.pallas_call(
        functools.partial(body, nd, nh, factor),
        out_shape=[
            shape(skip.shape, BF16),
            shape(skip.shape, BF16),
            shape((nh, tall, 128), F32),
            shape((tall, taps), F32),
            shape((round_up(ncj, 8), taps), F32),
            shape((round_up(nch, 8), taps), F32),
        ],
        in_specs=[pl.BlockSpec(memory_space=pltpu.VMEM)] + [pl.BlockSpec(memory_space=pl.ANY)] * 5,
        out_specs=[pl.BlockSpec(memory_space=pltpu.VMEM)] * 6,
        scratch_shapes=scratch,
        compiler_params=pltpu.CompilerParams(
            collective_id=0, has_side_effects=True, vmem_limit_bytes=56 * 1024 * 1024
        ),
        name="decoder",
    )(bottom[0].transpose(2, 0, 1), skip, upw, w1, w2, cotangent)
    result, gskip, cgrows, sumup, sumfirst, sumsecond = left
    anywhere = pl.BlockSpec(memory_space=pl.ANY)
    inside = pl.BlockSpec(memory_space=pltpu.VMEM)
    outs = pl.pallas_call(
        functools.partial(closing, nh),
        out_shape=[
            shape(skip.shape, BF16),
            shape((cb, nh, cw), BF16),
            shape(skip.shape, BF16),
            shape((27, no, cb), F32),
            shape((27, no, ncj), F32),
            shape((27, nch, no), F32),
        ],
        in_specs=[anywhere] * 2 + [inside] * 4,
        out_specs=[anywhere, inside, anywhere, inside, inside, inside],
        scratch_shapes=[pltpu.SemaphoreType.DMA((2,))],
        name="closing",
    )(result, gskip, cgrows.reshape(nh * tall, 128), sumup, sumfirst, sumsecond)
    return (
        outs[0],
        outs[1].transpose(1, 2, 0)[None],
        outs[2],
        outs[3].reshape(3, 3, 3, no, cb).transpose(0, 1, 2, 4, 3),
        outs[4].reshape(3, 3, 3, no, ncj).transpose(0, 1, 2, 4, 3),
        outs[5].reshape(3, 3, 3, nch, no),
    )


def solution(mesh):
    return jax.shard_map(
        functools.partial(per_device, mesh.shape["depth"], mesh.shape["height"]),
        mesh=mesh,
        in_specs=(
            P("depth", None, None, "height"),
            P("depth", "height", None, None),
            P(),
            P(),
            P(),
            P("depth", "height", None, None),
        ),
        out_specs=(
            P("depth", "height", None, None),
            P("depth", None, None, "height"),
            P("depth", "height", None, None),
            P(None, None, None, "height", "depth"),
            P(None, None, None, "height", "depth"),
            P(None, None, None, "height", "depth"),
        ),
        check_vma=False,
    )
```

time: 130 us -> 99.6 us (0.77)
  Pallas kernels: 118 us -> 98.3 us
  local copies, waits for them, and re-layouts: 11.5 us -> 0 us
    pallas_call x1 -> x2, Pallas kernels: 118 us -> 98.3 us  [the longest x1 91.5 us: per_device(): pl.pallas_call(functools.partial(body, nd, nh, factor), out_shape=[shape(...]
    unnamed x7 -> x0, local copies, waits for them, and re-layouts: 11.5 us -> none
where the time goes in v2:
time: 99.6 us; the launch traced here: 99 us
  Pallas kernels  98.3 us (99%)
    pallas_call x1, Pallas kernels, per_device(): pl.pallas_call(functools.partial(body, nd, nh, factor), out_shape=[shape(...  91.5 us
    pallas_call x1, Pallas kernels, per_device(): pl.pallas_call(functools.partial(closing, nh), out_shape=[shape(skip.shap...  6.79 us

profile of v2, /device:TPU:1, one launch (start us, length us, event | category | flops | bytes accessed | tf_op | source)
XLA Modules:
  0.0 99.0 jit_solution(1435124954540567987)
XLA Ops:
  0.6 91.5 %decoder.1 = (bf16[2,2,64,128]{3,2,1,0:T(8,128)(2,1)}, bf16[2,2,64,128]{3,2,1,0:T(8,128)(2,1)}, f32[16,24,128]{2,1,0:T(8,128)}, f32[24,256]{1,0:T(8,128)}, f32[16,256]{1,0:T(8,128)}, /*index=5*/f32[8,256]{1,0:T(8,128)}) custom-call(bf16[20,16,32]{2,1,0:T(8,128)(2,1)} %bitcast.21, bf16[2,2,64,128]{3,2,1,0:T(8,128)(2,1)} %skip.1, ...), custom_call_target="tpu_custom_call" | custom-call | tf_op jit(solution)/shard_map/decoder/pallas_call | solution.py:629
  92.2 6.8 %closing.1 = (bf16[2,2,64,128]{3,2,1,0:T(8,128)(2,1)}, bf16[20,16,32]{2,1,0:T(8,128)(2,1)}, bf16[2,2,64,128]{3,2,1,0:T(8,128)(2,1)}, f32[27,8,20]{2,1,0:T(8,128)...) custom-call(bf16[2,2,64,128]{3,2,1,0:T(8,128)(2,1)} %get-tuple-element.18.result, ...), custom_call_target="tpu_custom_call" | custom-call | tf_op jit(solution)/shard_map/closing/pallas_call | solution.py:650

commit v3 on v2

--- a/solution.py
+++ b/solution.py
@@ -113,9 +113,9 @@
 
 def body(
     nd, nh, factor,
-    bottom, skip, upw_hbm, w1_hbm, w2_hbm, cot_hbm,
-    result, gskip, cgrows, sumup, sumfirst, sumsecond,
-    upw, w1, w2, cot, bott, bsend, brecv, near, bg, up32, joined, jg, fp, hid, hg, e2, e1, et2s, et2r, et1s, et1r,
+    bottom_hbm, skip, upw_hbm, w1_hbm, w2_hbm, cot_hbm,
+    result_hbm, gskip_hbm, cgrows, sumup_hbm, sumfirst_hbm, sumsecond_hbm,
+    bottom, result, gskip, sumup, sumfirst, sumsecond, upw, w1, w2, cot, bott, bsend, brecv, near, bg, up32, joined, ug, sg, fp, hid, hg, e2, e1, et2s, et2r, et1s, et1r,
     bu32, bu, buts, butr, cgs, cgr, acc1, acc2, px2, pr2, px1, pr1, pxu, pru, gs2, gr2, gs1, gr1, gsu, gru,
     ssem, rsem, hs, hr, loc,
 ):
@@ -137,16 +137,20 @@
         pltpu.make_async_copy(cot_hbm, cot, loc.at[3]),
     ]
     own_skip = pltpu.make_async_copy(skip, joined.at[pl.ds(1, 2), pl.ds(1, 2), :, pl.ds(cu, cu)], loc.at[4])
-
+    own_gathered = pltpu.make_async_copy(skip, sg.at[pair], loc.at[6])
+
+    own_bottom = pltpu.make_async_copy(bottom_hbm, bottom, loc.at[5])
+    own_bottom.start()
+    for copy in weights:
+        copy.start()
     joined[...] = jnp.zeros_like(joined)
+    own_skip.start()
+    own_gathered.start()
     hid[...] = jnp.zeros_like(hid)
     e2[...] = jnp.zeros_like(e2)
     e1[...] = jnp.zeros_like(e1)
     bu[...] = jnp.zeros_like(bu)
 
-    own_skip.start()
-    for copy in weights:
-        copy.start()
 
     barrier = pltpu.get_barrier_semaphore()
 
@@ -173,6 +177,7 @@
             target = (lax.rem(d + dd + nd, nd), lax.rem(h + dh + nh, nh))
             pl.semaphore_signal(barrier, inc=1, device_id=target, device_id_type=MESH)
 
+    own_bottom.wait()
     bott[...] = bottom[...].astype(F32).reshape(cb * rows_all, cw)
     lines = [bott[pl.ds(r, cb, stride=rows_all), :] for r in range(rows_all)]
     blank = jnp.zeros((cb, cw), F32)
@@ -235,6 +240,8 @@
         ),
     )
     skip_halo.start()
+    skip_out = line_p(17, lambda p: skip, lambda s: sg.at[s])
+    skip_out.start()
     rows_out.wait_recv()
     stack = [brecv[c].astype(F32)[:cb] for c in range(nh)]
     wide = near.shape[3]
@@ -338,9 +345,9 @@
     hid_halo = field_halo(2, hid)
     hid_halo.start()
     hg[pair] = hidden
-    jg[pair] = joined[1:3, 1:3].reshape(cells, 2 * cu)
-    joined_out = line_p(4, lambda p: jg.at[pair], lambda s: jg.at[s])
-    joined_out.start()
+    ug[pair] = joined[1:3, 1:3, :, 0:cu].reshape(cells, cu)
+    up_out = line_p(4, lambda p: ug.at[pair], lambda s: ug.at[s])
+    up_out.start()
 
     weights[2].wait()
     weights[3].wait()
@@ -349,6 +356,8 @@
     result[...] = (second_pre * jax.nn.sigmoid(second_pre)).astype(BF16).reshape(2, 2, 2 * cw, cu)
     err2 = (cot[...].reshape(cells, cu).astype(F32) * slope(second_pre)).astype(BF16)
     e2[1:3, 1:3] = err2.reshape(2, 2, 2 * cw, cu)
+    out_result = pltpu.make_async_copy(result, result_hbm, loc.at[7])
+    out_result.start()
     e2_halo = field_halo(3, e2)
     e2_halo.start()
     hid_out = line_p(3, lambda p: hg.at[pair], lambda s: hg.at[s])
@@ -393,6 +402,8 @@
     bu_out = flip(bu[1:3, 1:3].reshape(cells, cu), 7, buts, butr)
     e1_out = flip(e1[...].reshape(4 * cells, cu), 8, et1s, et1r)
     gskip[...] = back[:, cu:].astype(BF16).reshape(2, 2, 2 * cw, cu)
+    out_gskip = pltpu.make_async_copy(gskip, gskip_hbm, loc.at[8])
+    out_gskip.start()
 
     def weight_grad(into, gathered, acc):
         acc[...] = jnp.zeros_like(acc)
@@ -420,7 +431,7 @@
                     for k in range(9):
                         pieces = [shifted[2 - kd + q][k][c * no : (c + 1) * no] for q in range(2)]
                         lhs.append(jnp.concatenate(pieces, axis=1))
-            acc[...] += dot(jnp.concatenate(lhs, axis=0).astype(BF16), gathered[j])
+            acc[...] += dot(jnp.concatenate(lhs, axis=0).astype(BF16), gathered(j))
             return carry
 
         lax.fori_loop(0, npair, step, 0)
@@ -465,7 +476,7 @@
 
     e2_out.wait_recv()
     hid_out.wait_recv()
-    swap2 = swap(9, weight_grad(et2r, hg, acc2), px2, pr2)
+    swap2 = swap(9, weight_grad(et2r, lambda j: hg[j], acc2), px2, pr2)
 
     bu_halo.wait_recv()
     around = lambda par: [bu[a, b, par].reshape(cw, cu) for a, b in GRID9]
@@ -477,8 +488,10 @@
     lhs = jnp.concatenate(around(1), axis=1)
     rhs = jnp.concatenate([upw[(a * 3 + b) * 3] for a, b in GRID9], axis=1)
     block_grad = flipped(same + shift_rows(dot(lhs, rhs, NT), 1, cw))
+    share = cb // (128 // cw)
     for c in range(nh):
-        cgs[c, 0:cb] = block_grad[c * cb : (c + 1) * cb]
+        groups = [block_grad[c * cb + q : c * cb + q + share, :cw] for q in range(0, cb, share)]
+        cgs[c, 0:share] = jnp.concatenate(groups, axis=1)
     cgr[h] = cgs[h]
     cg_out = line_h(10, lambda p: cgs.at[p], lambda s: cgr.at[s])
     cg_out.start()
@@ -527,23 +540,31 @@
     swapu = swap(12, grad_up, pxu, pru)
 
     e1_out.wait_recv()
-    joined_out.wait_recv()
-    swap1 = swap(13, weight_grad(et1r, jg, acc1), px1, pr1)
+    up_out.wait_recv()
+    skip_out.wait_recv()
+    own_gathered.wait()
+    swap1 = swap(13, weight_grad(et1r, lambda j: jnp.concatenate([ug[j], sg[j].reshape(cells, cu)], axis=1), acc1), px1, pr1)
     gu_out = scatter_rows(14, swapu, pru, cb, gsu, gru)
     g1_out = scatter_rows(15, swap1, pr1, 2 * cu // nh, gs1, gr1)
 
-    def finish(spread, into, out):
+    def finish(spread, into, out, hbm, at):
         spread.wait_recv()
         total = into[0].astype(F32)
         for s in range(1, nh):
             total = total + into[s].astype(F32)
         out[...] = total[: out.shape[0]]
-
-    finish(g2_out, gr2, sumsecond)
+        copy = pltpu.make_async_copy(out, hbm, loc.at[at])
+        copy.start()
+        return copy
+
+    finished = [finish(g2_out, gr2, sumsecond, sumsecond_hbm, 9)]
     cg_out.wait_recv()
-    cgrows[...] = cgr[...]
-    finish(gu_out, gru, sumup)
-    finish(g1_out, gr1, sumfirst)
+    out_cg = pltpu.make_async_copy(cgr, cgrows, loc.at[10])
+    out_cg.start()
+    finished.append(finish(gu_out, gru, sumup, sumup_hbm, 11))
+    finished.append(finish(g1_out, gr1, sumfirst, sumfirst_hbm, 12))
+    for copy in finished + [out_cg, out_result, out_gskip]:
+        copy.wait()
 
     for part in log:
         if not part.arrived:
@@ -551,26 +572,46 @@
         part.wait_send()
 
 
-def closing(nh, result, gskip, cgrows, sumup, sumfirst, sumsecond, out0, out1, out2, out3, out4, out5, sems):
-    whole = [pltpu.make_async_copy(result, out0, sems.at[0]), pltpu.make_async_copy(gskip, out2, sems.at[1])]
-    for copy in whole:
+def closing(nh, *refs):
+    (result, gskip, *left), (out0, out1h, out2, *grads), (cgrows, sumup, sumfirst, sumsecond) = (
+        refs[:6], refs[6:12], refs[12:16]
+    )
+    out1, out3, out4, out5, sems = refs[16:]
+    stages = (cgrows, sumup, sumfirst, sumsecond)
+    into = [pltpu.make_async_copy(src, dst, sems.at[i]) for i, (src, dst) in enumerate(zip(left, stages))]
+    whole = [pltpu.make_async_copy(result, out0, sems.at[4]), pltpu.make_async_copy(gskip, out2, sems.at[5])]
+    for copy in into + whole:
         copy.start()
-    cb = out1.shape[0]
+    cb, rows, cw = out1.shape
     tall = cgrows.shape[0] // nh
-    for c in range(cb):
-        out1[c] = cgrows[pl.ds(c, nh, stride=tall), 0 : out1.shape[2]].astype(BF16)
+    per = 128 // cw
+    share = cb // per
+    away = [
+        pltpu.make_async_copy(src, dst, sems.at[6 + i])
+        for i, (src, dst) in enumerate(zip((out1, out3, out4, out5), [out1h] + grads))
+    ]
+    into[0].wait()
+    for i in range(share):
+        line = cgrows[pl.ds(i, nh, stride=tall), :].astype(BF16)
+        for q in range(per):
+            out1[q * share + i] = line[:, q * cw : (q + 1) * cw]
+    away[0].start()
     no = out3.shape[1]
-    for total, out in ((sumup, out3), (sumfirst, out4)):
+    for k, (total, out) in enumerate(((sumup, out3), (sumfirst, out4))):
+        into[1 + k].wait()
         n = out.shape[2]
         turned = total[...]
         if turned.shape[0] < 128:
             fill = jnp.zeros((128 - turned.shape[0], turned.shape[1]), F32)
             turned = jnp.concatenate([turned, fill], axis=0)
         out[...] = turned.T[: 27 * no, :n].reshape(27, no, n)
+        away[1 + k].start()
+    into[3].wait()
     total = sumsecond[...]
     for t in range(27):
         out5[t] = total[: out5.shape[1], t * no : (t + 1) * no]
-    for copy in whole:
+    away[3].start()
+    for copy in whole + away:
         copy.wait()
 
 
@@ -593,7 +634,10 @@
     line = max(nd, nh)
     wide = round_up(cin, 128)
     part = 27 * no
+    tall = round_up(cb * cw // 128, 8)
     scratch = [
+        v((cb, nh, cw), BF16), v(skip.shape, BF16), v(skip.shape, BF16),
+        v((round_up(cb, 8), taps), F32), v((round_up(ncj, 8), taps), F32), v((round_up(nch, 8), taps), F32),
         v(upw.shape, BF16), v(w1.shape, BF16), v(w2.shape, BF16), v(cotangent.shape, BF16),
         v((cb * nh, cw), F32),
         v((nh, round_up(cb, 16), 128), BF16), v((nh, round_up(cb, 16), 128), BF16),
@@ -601,7 +645,8 @@
         v((npair, 2, 2, cw, wide), BF16),
         v((4, 4, fw, cu), F32),
         v((4, 4, fw, cj), BF16),
-        v((npair, cells, cj), BF16),
+        v((npair, cells, cu), BF16),
+        v((npair,) + skip.shape, BF16),
         v((cells, cu), F32),
         v((4, 4, fw, cu), BF16),
         v((npair, cells, cu), BF16),
@@ -612,7 +657,7 @@
         v((2, 2, fw, cu), F32),
         v((3, 3, 2, cw, cu), BF16),
         v((cu, cells), BF16), v((npair, both, cells), BF16),
-        v((nh, round_up(cb, 8), 128), F32), v((nh, round_up(cb, 8), 128), F32),
+        v((nh, tall, 128), F32), v((nh, tall, 128), F32),
         v((2 * part, cj), F32), v((2 * part, cu), F32),
         v((part, cu), F32), v((part, cu), F32),
         v((part, cj), F32), v((part, cj), F32),
@@ -620,48 +665,39 @@
         v((nh, round_up(nch, 8), taps), F32), v((nh, round_up(nch, 8), taps), F32),
         v((nh, round_up(ncj, 16), taps), BF16), v((nh, round_up(ncj, 16), taps), BF16),
         v((nh, round_up(cb, 16), taps), BF16), v((nh, round_up(cb, 16), taps), BF16),
-        pltpu.SemaphoreType.DMA((16, line)), pltpu.SemaphoreType.DMA((16, line)),
+        pltpu.SemaphoreType.DMA((18, line)), pltpu.SemaphoreType.DMA((18, line)),
         pltpu.SemaphoreType.DMA((6, 9)), pltpu.SemaphoreType.DMA((6, 9)),
-        pltpu.SemaphoreType.DMA((6,)),
+        pltpu.SemaphoreType.DMA((13,)),
     ]
-    tall = round_up(cb, 8)
     shape = jax.ShapeDtypeStruct
+    anywhere = pl.BlockSpec(memory_space=pl.ANY)
+    tops = [
+        shape((nh, tall, 128), F32),
+        shape((round_up(cb, 8), taps), F32),
+        shape((round_up(ncj, 8), taps), F32),
+        shape((round_up(nch, 8), taps), F32),
+    ]
     left = pl.pallas_call(
         functools.partial(body, nd, nh, factor),
-        out_shape=[
-            shape(skip.shape, BF16),
-            shape(skip.shape, BF16),
-            shape((nh, tall, 128), F32),
-            shape((tall, taps), F32),
-            shape((round_up(ncj, 8), taps), F32),
-            shape((round_up(nch, 8), taps), F32),
-        ],
-        in_specs=[pl.BlockSpec(memory_space=pltpu.VMEM)] + [pl.BlockSpec(memory_space=pl.ANY)] * 5,
-        out_specs=[pl.BlockSpec(memory_space=pltpu.VMEM)] * 6,
+        out_shape=[shape(skip.shape, BF16), shape(skip.shape, BF16)] + tops,
+        in_specs=[anywhere] * 6,
+        out_specs=[anywhere] * 6,
         scratch_shapes=scratch,
         compiler_params=pltpu.CompilerParams(
             collective_id=0, has_side_effects=True, vmem_limit_bytes=56 * 1024 * 1024
         ),
         name="decoder",
     )(bottom[0].transpose(2, 0, 1), skip, upw, w1, w2, cotangent)
-    result, gskip, cgrows, sumup, sumfirst, sumsecond = left
-    anywhere = pl.BlockSpec(memory_space=pl.ANY)
-    inside = pl.BlockSpec(memory_space=pltpu.VMEM)
+    tops[0] = shape((nh * tall, 128), F32)
+    ends = [shape((cb, nh, cw), BF16), shape((27, no, cb), F32), shape((27, no, ncj), F32), shape((27, nch, no), F32)]
     outs = pl.pallas_call(
         functools.partial(closing, nh),
-        out_shape=[
-            shape(skip.shape, BF16),
-            shape((cb, nh, cw), BF16),
-            shape(skip.shape, BF16),
-            shape((27, no, cb), F32),
-            shape((27, no, ncj), F32),
-            shape((27, nch, no), F32),
-        ],
-        in_specs=[anywhere] * 2 + [inside] * 4,
-        out_specs=[anywhere, inside, anywhere, inside, inside, inside],
-        scratch_shapes=[pltpu.SemaphoreType.DMA((2,))],
+        out_shape=[shape(skip.shape, BF16), ends[0], shape(skip.shape, BF16)] + ends[1:],
+        in_specs=[anywhere] * 6,
+        out_specs=[anywhere] * 6,
+        scratch_shapes=[v(one.shape, one.dtype) for one in tops + ends] + [pltpu.SemaphoreType.DMA((10,))],
         name="closing",
-    )(result, gskip, cgrows.reshape(nh * tall, 128), sumup, sumfirst, sumsecond)
+    )(*left[:2], left[2].reshape(nh * tall, 128), *left[3:])
     return (
         outs[0],
         outs[1].transpose(1, 2, 0)[None],

time: 99.6 us -> 93.8 us (0.942)
  Pallas kernels: 98.3 us -> 93 us
    pallas_call x1, Pallas kernels: 91.5 us -> 87.9 us  [per_device(): pl.pallas_call(functools.partial(body, nd, nh, factor), out_shape=[shape(...]
    pallas_call x1, Pallas kernels: 6.79 us -> 5.17 us  [per_device(): pl.pallas_call(functools.partial(closing, nh), out_shape=[shape(skip.shap...]
where the time goes in v3:
time: 93.8 us; the launch traced here: 93.7 us
  Pallas kernels  93 us (99%)
    pallas_call x1, Pallas kernels, per_device(): pl.pallas_call(functools.partial(body, nd, nh, factor), out_shape=[shape(...  87.9 us
    pallas_call x1, Pallas kernels, per_device(): pl.pallas_call(functools.partial(closing, nh), out_shape=[shape(skip.shap...  5.17 us

profile of v3, /device:TPU:1, one launch (start us, length us, event | category | flops | bytes accessed | tf_op | source)
XLA Modules:
  0.0 93.7 jit_solution(17589632099709314813)
XLA Ops:
  0.6 87.9 %decoder.1 = (bf16[2,2,64,128]{3,2,1,0:T(8,128)(2,1)}, bf16[2,2,64,128]{3,2,1,0:T(8,128)(2,1)}, f32[16,8,128]{2,1,0:T(8,128)}, f32[24,256]{1,0:T(8,128)}, f32[16,256]{1,0:T(8,128)}, /*index=5*/f32[8,256]{1,0:T(8,128)}) custom-call(bf16[20,16,32]{2,1,0:T(8,128)(2,1)} %bitcast.20, bf16[2,2,64,128]{3,2,1,0:T(8,128)(2,1)} %skip.1, ...), custom_call_target="tpu_custom_call" | custom-call | tf_op jit(solution)/shard_map/decoder/pallas_call | solution.py:680
  88.5 5.2 %closing.1 = (bf16[2,2,64,128]{3,2,1,0:T(8,128)(2,1)}, bf16[20,16,32]{2,1,0:T(8,128)(2,1)}, bf16[2,2,64,128]{3,2,1,0:T(8,128)(2,1)}, f32[27,8,20]{2,1,0:T(8,128)...) custom-call(bf16[2,2,64,128]{3,2,1,0:T(8,128)(2,1)} %get-tuple-element.18.refs_0_, ...), custom_call_target="tpu_custom_call" | custom-call | tf_op jit(solution)/shard_map/closing/pallas_call | solution.py:693

commit v4 on v3

--- a/solution.py
+++ b/solution.py
@@ -240,7 +240,8 @@
         ),
     )
     skip_halo.start()
-    skip_out = line_p(17, lambda p: skip, lambda s: sg.at[s])
+    skip_out = line_p(17, lambda p: sg.at[pair], lambda s: sg.at[s])
+    own_gathered.wait()
     skip_out.start()
     rows_out.wait_recv()
     stack = [brecv[c].astype(F32)[:cb] for c in range(nh)]
@@ -253,6 +254,10 @@
     plane_prev = line_d(2, lambda p: near.at[1], lambda s: near.at[2], (nd - 1, nd))
     plane_next.start()
     plane_prev.start()
+    bg[core, pair] = near[1, 1:3]
+    bg[0, npair] = jnp.zeros_like(near[1, 1:3])
+    planes_out = line_p(6, lambda p: bg.at[core, pair], lambda s: bg.at[core, s])
+    planes_out.start()
     weights[0].wait()
     plane_next.wait_recv()
     plane_prev.wait_recv()
@@ -264,7 +269,6 @@
         value = near[s, :, :, 0:cin]
         coarse.append(jnp.where(here, value, jnp.zeros_like(value)))
     coarse = jnp.stack(coarse)
-    bg[pair] = jnp.stack([near[1, 1:3], jnp.where(d < nd - 1, near[2, 1:3], jnp.zeros_like(near[2, 1:3]))])
     first_of = {0: 1, 1: 1, 2: 0}
     for gd in range(2):
         for gh in range(2):
@@ -380,8 +384,13 @@
         return spread
 
     e2_out = flip(e2[...].reshape(4 * cells, cu), 5, et2s, et2r)
-    planes_out = line_p(6, lambda p: bg.at[pair], lambda s: bg.at[s])
-    planes_out.start()
+
+    def swap_copy(phase, src, dst, arriving):
+        copy = Spread(log, 0, 2, None, None, None, None, None)
+        sems = ssem.at[phase, 0], rsem.at[phase, 0]
+        copy.outgoing = lambda j: remote(src, dst, *sems, (partner, h))
+        copy.incoming = lambda j: remote(src, arriving, *sems, (partner, h))
+        return copy
 
     e1_halo.wait_recv()
     back = conv_back(e1, w1)
@@ -401,6 +410,9 @@
     bu_halo.start()
     bu_out = flip(bu[1:3, 1:3].reshape(cells, cu), 7, buts, butr)
     e1_out = flip(e1[...].reshape(4 * cells, cu), 8, et1s, et1r)
+    planes_out.wait_recv()
+    planes_swap = swap_copy(16, bg.at[core, pl.ds(0, npair)], bg.at[core, pl.ds(0, npair)], bg.at[1 - core, pl.ds(0, npair)])
+    planes_swap.start()
     gskip[...] = back[:, cu:].astype(BF16).reshape(2, 2, 2 * cw, cu)
     out_gskip = pltpu.make_async_copy(gskip, gskip_hbm, loc.at[8])
     out_gskip.start()
@@ -442,11 +454,7 @@
         halves = [value[:half], value[half:]]
         mine = jnp.where(core == 0, halves[0], halves[1])
         out[...] = jnp.where(core == 0, halves[1], halves[0])
-        copy = line_d(phase, lambda p: out, lambda s: into, (1, 2))
-        copy.target = lambda p: (partner, h)
-        copy.outgoing = copy.incoming = lambda j: remote(
-            out, into, ssem.at[phase, 0], rsem.at[phase, 0], (partner, h)
-        )
+        copy = swap_copy(phase, out, into, into)
         copy.start()
         return copy, mine
 
@@ -522,13 +530,15 @@
         value = phases[PARITY_SHIFT[kd][0], PARITY_SHIFT[kh][0], pw]
         return shift_lanes(value, 1, cw) if sw else value
 
-    planes_out.wait_recv()
+    planes_swap.wait_recv()
     products = {}
     for sd, kds in ((0, (1, 2)), (1, (0,))):
         for sh, khs in ((0, (1, 2)), (1, (0,))):
             order = [(kd, kh, kw) for kd in kds for kh in khs for kw in range(3)]
             lhs = jnp.concatenate([tap_rows(*k) for k in order], axis=0).astype(BF16)
-            rhs = bg[:, sd, sh].reshape(span, -1)
+            odd_one = lax.rem(core + sd, 2)
+            first = core * sd
+            rhs = bg[odd_one, pl.ds(first, npair), sh].reshape(span, -1)
             value = dot(lhs, rhs)
             for i, k in enumerate(order):
                 for c in range(2):
@@ -542,7 +552,6 @@
     e1_out.wait_recv()
     up_out.wait_recv()
     skip_out.wait_recv()
-    own_gathered.wait()
     swap1 = swap(13, weight_grad(et1r, lambda j: jnp.concatenate([ug[j], sg[j].reshape(cells, cu)], axis=1), acc1), px1, pr1)
     gu_out = scatter_rows(14, swapu, pru, cb, gsu, gru)
     g1_out = scatter_rows(15, swap1, pr1, 2 * cu // nh, gs1, gr1)
@@ -576,11 +585,12 @@
     (result, gskip, *left), (out0, out1h, out2, *grads), (cgrows, sumup, sumfirst, sumsecond) = (
         refs[:6], refs[6:12], refs[12:16]
     )
-    out1, out3, out4, out5, sems = refs[16:]
+    out1, out3, out4, out5, pass0, pass1, sems = refs[16:]
     stages = (cgrows, sumup, sumfirst, sumsecond)
     into = [pltpu.make_async_copy(src, dst, sems.at[i]) for i, (src, dst) in enumerate(zip(left, stages))]
-    whole = [pltpu.make_async_copy(result, out0, sems.at[4]), pltpu.make_async_copy(gskip, out2, sems.at[5])]
-    for copy in into + whole:
+    through = [pltpu.make_async_copy(result, pass0, sems.at[4]), pltpu.make_async_copy(gskip, pass1, sems.at[5])]
+    whole = [pltpu.make_async_copy(pass0, out0, sems.at[10]), pltpu.make_async_copy(pass1, out2, sems.at[11])]
+    for copy in into + through:
         copy.start()
     cb, rows, cw = out1.shape
     tall = cgrows.shape[0] // nh
@@ -596,6 +606,9 @@
         for q in range(per):
             out1[q * share + i] = line[:, q * cw : (q + 1) * cw]
     away[0].start()
+    for arriving, leaving in zip(through, whole):
+        arriving.wait()
+        leaving.start()
     no = out3.shape[1]
     for k, (total, out) in enumerate(((sumup, out3), (sumfirst, out4))):
         into[1 + k].wait()
@@ -642,7 +655,7 @@
         v((cb * nh, cw), F32),
         v((nh, round_up(cb, 16), 128), BF16), v((nh, round_up(cb, 16), 128), BF16),
         v((3, 3, cw, wide), BF16),
-        v((npair, 2, 2, cw, wide), BF16),
+        v((2, npair + 1, 2, cw, wide), BF16),
         v((4, 4, fw, cu), F32),
         v((4, 4, fw, cj), BF16),
         v((npair, cells, cu), BF16),
@@ -695,7 +708,8 @@
         out_shape=[shape(skip.shape, BF16), ends[0], shape(skip.shape, BF16)] + ends[1:],
         in_specs=[anywhere] * 6,
         out_specs=[anywhere] * 6,
-        scratch_shapes=[v(one.shape, one.dtype) for one in tops + ends] + [pltpu.SemaphoreType.DMA((10,))],
+        scratch_shapes=[v(one.shape, one.dtype) for one in tops + ends]
+        + [v(skip.shape, BF16), v(skip.shape, BF16), pltpu.SemaphoreType.DMA((12,))],
         name="closing",
     )(*left[:2], left[2].reshape(nh * tall, 128), *left[3:])
     return (

time: 93.8 us -> 83 us (0.88)
  Pallas kernels: 93 us -> 82.2 us
    pallas_call x1, Pallas kernels: 87.9 us -> 80.2 us  [per_device(): pl.pallas_call(functools.partial(body, nd, nh, factor), out_shape=[shape(...]
    pallas_call x1, Pallas kernels: 5.17 us -> 2.01 us  [per_device(): pl.pallas_call(functools.partial(closing, nh), out_shape=[shape(skip.shap...]
where the time goes in v4:
time: 83 us; the launch traced here: 82.8 us
  Pallas kernels  82.2 us (99%)
    pallas_call x1, Pallas kernels, per_device(): pl.pallas_call(functools.partial(body, nd, nh, factor), out_shape=[shape(...  80.2 us
    pallas_call x1, Pallas kernels, per_device(): pl.pallas_call(functools.partial(closing, nh), out_shape=[shape(skip.shap...  2.01 us

profile of v4, /device:TPU:1, one launch (start us, length us, event | category | flops | bytes accessed | tf_op | source)
XLA Modules:
  0.0 82.8 jit_solution(14023119583599502872)
XLA Ops:
  0.6 80.2 %decoder.1 = (bf16[2,2,64,128]{3,2,1,0:T(8,128)(2,1)}, bf16[2,2,64,128]{3,2,1,0:T(8,128)(2,1)}, f32[16,8,128]{2,1,0:T(8,128)}, f32[24,256]{1,0:T(8,128)}, f32[16,256]{1,0:T(8,128)}, /*index=5*/f32[8,256]{1,0:T(8,128)}) custom-call(bf16[20,16,32]{2,1,0:T(8,128)(2,1)} %bitcast.20, bf16[2,2,64,128]{3,2,1,0:T(8,128)(2,1)} %skip.1, ...), custom_call_target="tpu_custom_call" | custom-call | tf_op jit(solution)/shard_map/decoder/pallas_call | solution.py:693
  80.8 2.0 %closing.1 = (bf16[2,2,64,128]{3,2,1,0:T(8,128)(2,1)}, bf16[20,16,32]{2,1,0:T(8,128)(2,1)}, bf16[2,2,64,128]{3,2,1,0:T(8,128)(2,1)}, f32[27,8,20]{2,1,0:T(8,128)...) custom-call(bf16[2,2,64,128]{3,2,1,0:T(8,128)(2,1)} %get-tuple-element.18.refs_0_, ...), custom_call_target="tpu_custom_call" | custom-call | tf_op jit(solution)/shard_map/closing/pallas_call | solution.py:706

commit v5 on v4

--- a/solution.py
+++ b/solution.py
@@ -28,41 +28,48 @@
 
 
 class Spread:
-    def __init__(self, log, me, count, target, source, slot, send, recv, steps=None):
+    def __init__(self, log, me, count, target, source, slot, bulk, send, recv):
         self.me, self.count, self.target = me, count, target
-        self.source, self.slot, self.send, self.recv = source, slot, send, recv
-        self.steps = steps or (1, count)
+        self.source, self.slot, self.bulk, self.send, self.recv = source, slot, bulk, send, recv
         self.arrived, self.log = False, log
-
-    def each(self, act):
-        def step(j, carry):
-            act(j)
-            return carry
-
-        lax.fori_loop(*self.steps, step, 0)
-
-    def outgoing(self, j):
-        peer = lax.rem(self.me + j, self.count)
-        return remote(
-            self.source(peer), self.slot(self.me), self.send.at[peer], self.recv.at[self.me], self.target(peer)
-        )
-
-    def incoming(self, j):
-        peer = lax.rem(self.me + self.count - j, self.count)
-        return remote(
-            self.source(peer), self.slot(peer), self.send.at[peer], self.recv.at[peer], self.target(peer)
-        )
 
     def start(self):
         self.log.append(self)
-        self.each(lambda j: self.outgoing(j).start())
+
+        def step(j, carry):
+            peer = lax.rem(self.me + j, self.count)
+            remote(self.source(peer), self.slot(self.me), self.send, self.recv, self.target(peer)).start()
+            return carry
+
+        lax.fori_loop(1, self.count, step, 0)
+
+    def whole(self):
+        peer = lax.rem(self.me + 1, self.count)
+        return remote(self.bulk, self.bulk, self.send, self.recv, self.target(peer))
 
     def wait_recv(self):
         self.arrived = True
-        self.each(lambda j: self.incoming(j).wait_recv())
+        self.whole().wait_recv()
 
     def wait_send(self):
-        self.each(lambda j: self.outgoing(j).wait_send())
+        self.whole().wait_send()
+
+
+class Single:
+    def __init__(self, log, out, into):
+        self.out, self.into = out, into
+        self.arrived, self.log = False, log
+
+    def start(self):
+        self.log.append(self)
+        self.out.start()
+
+    def wait_recv(self):
+        self.arrived = True
+        self.into.wait_recv()
+
+    def wait_send(self):
+        self.out.wait_send()
 
 
 class Halo:
@@ -116,7 +123,7 @@
     bottom_hbm, skip, upw_hbm, w1_hbm, w2_hbm, cot_hbm,
     result_hbm, gskip_hbm, cgrows, sumup_hbm, sumfirst_hbm, sumsecond_hbm,
     bottom, result, gskip, sumup, sumfirst, sumsecond, upw, w1, w2, cot, bott, bsend, brecv, near, bg, up32, joined, ug, sg, fp, hid, hg, e2, e1, et2s, et2r, et1s, et1r,
-    bu32, bu, buts, butr, cgs, cgr, acc1, acc2, px2, pr2, px1, pr1, pxu, pru, gs2, gr2, gs1, gr1, gsu, gru,
+    bu32, bu, buts, butr, cgr, acc1, acc2, px2, pr2, px1, pr1, pxu, pru, gs2, gr2, gs1, gr1, gsu, gru,
     ssem, rsem, hs, hr, loc,
 ):
     d = lax.axis_index("depth")
@@ -219,18 +226,23 @@
             ),
         )
 
-    def line_h(phase, source, slot):
-        return Spread(log, h, nh, lambda p: (d, p), source, slot, ssem.at[phase], rsem.at[phase])
-
-    def line_d(phase, source, slot, steps):
-        return Spread(log, d, nd, lambda p: (p, h), source, slot, ssem.at[phase], rsem.at[phase], steps)
-
-    def line_p(phase, source, slot):
+    def line_h(phase, source, into):
         return Spread(
-            log, pair, npair, lambda p: (2 * p + core, h), source, slot, ssem.at[phase], rsem.at[phase]
+            log, h, nh, lambda p: (d, p), source, lambda s: into.at[s], into.at[pl.ds(0, nh - 1)],
+            ssem.at[phase], rsem.at[phase],
         )
 
-    rows_out = line_h(0, lambda p: bsend.at[p], lambda s: brecv.at[s])
+    def line_p(phase, source, into):
+        return Spread(
+            log, pair, npair, lambda p: (2 * p + core, h), source, lambda s: into.at[s],
+            into.at[pl.ds(0, npair - 1)], ssem.at[phase], rsem.at[phase],
+        )
+
+    def single(phase, src, dst, target, arriving):
+        sems = ssem.at[phase], rsem.at[phase]
+        return Single(log, remote(src, dst, *sems, target), remote(src, arriving, *sems, target))
+
+    rows_out = line_h(0, lambda p: bsend.at[p], brecv)
     rows_out.start()
     skip_halo = halo(
         0,
@@ -240,7 +252,7 @@
         ),
     )
     skip_halo.start()
-    skip_out = line_p(17, lambda p: sg.at[pair], lambda s: sg.at[s])
+    skip_out = line_p(17, lambda p: sg.at[pair], sg)
     own_gathered.wait()
     skip_out.start()
     rows_out.wait_recv()
@@ -250,13 +262,13 @@
         stack.append(jnp.zeros((wide - cin, 128), F32))
     near[1] = jnp.concatenate(stack, axis=0).T[: 3 * cw].reshape(3, cw, wide).astype(BF16)
 
-    plane_next = line_d(1, lambda p: near.at[1], lambda s: near.at[0], (1, 2))
-    plane_prev = line_d(2, lambda p: near.at[1], lambda s: near.at[2], (nd - 1, nd))
+    plane_next = single(1, near.at[1], near.at[0], (lax.rem(d + 1, nd), h), near.at[0])
+    plane_prev = single(2, near.at[1], near.at[2], (lax.rem(d + nd - 1, nd), h), near.at[2])
     plane_next.start()
     plane_prev.start()
     bg[core, pair] = near[1, 1:3]
     bg[0, npair] = jnp.zeros_like(near[1, 1:3])
-    planes_out = line_p(6, lambda p: bg.at[core, pair], lambda s: bg.at[core, s])
+    planes_out = line_p(6, lambda p: bg.at[core, pair], bg.at[core])
     planes_out.start()
     weights[0].wait()
     plane_next.wait_recv()
@@ -350,7 +362,7 @@
     hid_halo.start()
     hg[pair] = hidden
     ug[pair] = joined[1:3, 1:3, :, 0:cu].reshape(cells, cu)
-    up_out = line_p(4, lambda p: ug.at[pair], lambda s: ug.at[s])
+    up_out = line_p(4, lambda p: ug.at[pair], ug)
     up_out.start()
 
     weights[2].wait()
@@ -364,14 +376,8 @@
     out_result.start()
     e2_halo = field_halo(3, e2)
     e2_halo.start()
-    hid_out = line_p(3, lambda p: hg.at[pair], lambda s: hg.at[s])
+    hid_out = line_p(3, lambda p: hg.at[pair], hg)
     hid_out.start()
-
-    e2_halo.wait_recv()
-    err1 = (conv_back(e2, w2) * slope(fp[...])).astype(BF16)
-    e1[1:3, 1:3] = err1.reshape(2, 2, 2 * cw, cu)
-    e1_halo = field_halo(4, e1)
-    e1_halo.start()
 
     def part_of(p):
         return pl.ds(pl.multiple_of(p * both, both), both)
@@ -379,43 +385,9 @@
     def flip(value, phase, out, into):
         out[...] = value.astype(F32).T.astype(BF16)
         into[pair] = out[part_of(pair)]
-        spread = line_p(phase, lambda p: out.at[part_of(p)], lambda s: into.at[s])
+        spread = line_p(phase, lambda p: out.at[part_of(p)], into)
         spread.start()
         return spread
-
-    e2_out = flip(e2[...].reshape(4 * cells, cu), 5, et2s, et2r)
-
-    def swap_copy(phase, src, dst, arriving):
-        copy = Spread(log, 0, 2, None, None, None, None, None)
-        sems = ssem.at[phase, 0], rsem.at[phase, 0]
-        copy.outgoing = lambda j: remote(src, dst, *sems, (partner, h))
-        copy.incoming = lambda j: remote(src, arriving, *sems, (partner, h))
-        return copy
-
-    e1_halo.wait_recv()
-    back = conv_back(e1, w1)
-    bu32[...] = back[:, :cu].reshape(2, 2, 2 * cw, cu)
-    for i in range(2):
-        for j in range(2):
-            for par in range(2):
-                bu[1 + i, 1 + j, par] = bu32[i, j, pl.ds(par, cw, stride=2), :].astype(BF16)
-    bu_halo = halo(
-        5,
-        lambda dd, dh: (
-            bu.at[pl.ds(2, 1) if dd else pl.ds(1, 2), pl.ds(2, 1) if dh else pl.ds(1, 2)],
-            bu.at[pl.ds(0, 1) if dd else pl.ds(1, 2), pl.ds(0, 1) if dh else pl.ds(1, 2)],
-        ),
-        [(1, 0), (0, 1), (1, 1)],
-    )
-    bu_halo.start()
-    bu_out = flip(bu[1:3, 1:3].reshape(cells, cu), 7, buts, butr)
-    e1_out = flip(e1[...].reshape(4 * cells, cu), 8, et1s, et1r)
-    planes_out.wait_recv()
-    planes_swap = swap_copy(16, bg.at[core, pl.ds(0, npair)], bg.at[core, pl.ds(0, npair)], bg.at[1 - core, pl.ds(0, npair)])
-    planes_swap.start()
-    gskip[...] = back[:, cu:].astype(BF16).reshape(2, 2, 2 * cw, cu)
-    out_gskip = pltpu.make_async_copy(gskip, gskip_hbm, loc.at[8])
-    out_gskip.start()
 
     def weight_grad(into, gathered, acc):
         acc[...] = jnp.zeros_like(acc)
@@ -454,7 +426,7 @@
         halves = [value[:half], value[half:]]
         mine = jnp.where(core == 0, halves[0], halves[1])
         out[...] = jnp.where(core == 0, halves[1], halves[0])
-        copy = swap_copy(phase, out, into, into)
+        copy = single(phase, out, into, (partner, h), into)
         copy.start()
         return copy, mine
 
@@ -467,42 +439,68 @@
             value = jnp.concatenate([value, jnp.zeros((tall, wide - lanes), F32)], axis=1)
         return value.T
 
-    def scatter_rows(phase, swapped, arriving, chunk, out, into):
+    first_taps = 14
+    split = first_taps * no
+    lanes = round_up(split, 128)
+
+    def scatter_rows(phase, swapped, arriving, chunk, out, into, folded=True, beside=None):
         copy, mine = swapped
         copy.wait_recv()
         turned = flipped((mine + arriving[...]) * factor)
-        fill = out.shape[1] - chunk
         for c in range(nh):
             piece = turned[c * chunk : (c + 1) * chunk]
+            if folded:
+                piece = jnp.concatenate([piece[:, :lanes], piece[:, split : split + lanes]], axis=0)
+            if beside:
+                piece = jnp.concatenate([piece, beside[c]], axis=0)
+            fill = out.shape[1] - piece.shape[0]
             if fill:
                 piece = jnp.concatenate([piece, jnp.zeros((fill, piece.shape[1]), F32)], axis=0)
-            out[c] = piece.astype(out.dtype)
+            out[c] = piece.astype(BF16)
         into[h] = out[h]
-        spread = line_h(phase, lambda p: out.at[p], lambda s: into.at[s])
+        spread = line_h(phase, lambda p: out.at[p], into)
         spread.start()
         return spread
 
+    e2_halo.wait_recv()
+    err1 = (conv_back(e2, w2) * slope(fp[...])).astype(BF16)
+    e1[1:3, 1:3] = err1.reshape(2, 2, 2 * cw, cu)
+    e1_halo = field_halo(4, e1)
+    e1_halo.start()
+    e2_out = flip(e2[...].reshape(4 * cells, cu), 5, et2s, et2r)
+
+    e1_halo.wait_recv()
+    e1_out = flip(e1[...].reshape(4 * cells, cu), 8, et1s, et1r)
+    back = conv_back(e1, w1)
+    bu32[...] = back[:, :cu].reshape(2, 2, 2 * cw, cu)
+    for i in range(2):
+        for j in range(2):
+            for par in range(2):
+                bu[1 + i, 1 + j, par] = bu32[i, j, pl.ds(par, cw, stride=2), :].astype(BF16)
+    bu_halo = halo(
+        5,
+        lambda dd, dh: (
+            bu.at[pl.ds(2, 1) if dd else pl.ds(1, 2), pl.ds(2, 1) if dh else pl.ds(1, 2)],
+            bu.at[pl.ds(0, 1) if dd else pl.ds(1, 2), pl.ds(0, 1) if dh else pl.ds(1, 2)],
+        ),
+        [(1, 0), (0, 1), (1, 1)],
+    )
+    bu_halo.start()
+    bu_out = flip(bu[1:3, 1:3].reshape(cells, cu), 7, buts, butr)
     e2_out.wait_recv()
     hid_out.wait_recv()
     swap2 = swap(9, weight_grad(et2r, lambda j: hg[j], acc2), px2, pr2)
-
-    bu_halo.wait_recv()
-    around = lambda par: [bu[a, b, par].reshape(cw, cu) for a, b in GRID9]
-    lhs = jnp.concatenate(around(0) + around(1), axis=1)
-    rhs = jnp.concatenate(
-        [upw[(a * 3 + b) * 3 + 1] for a, b in GRID9] + [upw[(a * 3 + b) * 3 + 2] for a, b in GRID9], axis=1
-    )
-    same = dot(lhs, rhs, NT)
-    lhs = jnp.concatenate(around(1), axis=1)
-    rhs = jnp.concatenate([upw[(a * 3 + b) * 3] for a, b in GRID9], axis=1)
-    block_grad = flipped(same + shift_rows(dot(lhs, rhs, NT), 1, cw))
-    share = cb // (128 // cw)
-    for c in range(nh):
-        groups = [block_grad[c * cb + q : c * cb + q + share, :cw] for q in range(0, cb, share)]
-        cgs[c, 0:share] = jnp.concatenate(groups, axis=1)
-    cgr[h] = cgs[h]
-    cg_out = line_h(10, lambda p: cgs.at[p], lambda s: cgr.at[s])
-    cg_out.start()
+    planes_out.wait_recv()
+    planes_swap = single(
+        16, bg.at[core, pl.ds(0, npair)], bg.at[core, pl.ds(0, npair)], (partner, h), bg.at[1 - core, pl.ds(0, npair)]
+    )
+    planes_swap.start()
+
+    e1_out.wait_recv()
+    up_out.wait_recv()
+    skip_out.wait_recv()
+    swap1 = swap(13, weight_grad(et1r, lambda j: jnp.concatenate([ug[j], sg[j].reshape(cells, cu)], axis=1), acc1), px1, pr1)
+
     g2_out = scatter_rows(11, swap2, pr2, cu // nh, gs2, gr2)
 
     bu_out.wait_recv()
@@ -549,12 +547,26 @@
     )
     swapu = swap(12, grad_up, pxu, pru)
 
-    e1_out.wait_recv()
-    up_out.wait_recv()
-    skip_out.wait_recv()
-    swap1 = swap(13, weight_grad(et1r, lambda j: jnp.concatenate([ug[j], sg[j].reshape(cells, cu)], axis=1), acc1), px1, pr1)
-    gu_out = scatter_rows(14, swapu, pru, cb, gsu, gru)
-    g1_out = scatter_rows(15, swap1, pr1, 2 * cu // nh, gs1, gr1)
+    g1_out = scatter_rows(15, swap1, pr1, 2 * cu // nh, gs1, gr1, folded=False)
+    bu_halo.wait_recv()
+    around = lambda par: [bu[a, b, par].reshape(cw, cu) for a, b in GRID9]
+    lhs = jnp.concatenate(around(0) + around(1), axis=1)
+    rhs = jnp.concatenate(
+        [upw[(a * 3 + b) * 3 + 1] for a, b in GRID9] + [upw[(a * 3 + b) * 3 + 2] for a, b in GRID9], axis=1
+    )
+    same = dot(lhs, rhs, NT)
+    lhs = jnp.concatenate(around(1), axis=1)
+    rhs = jnp.concatenate([upw[(a * 3 + b) * 3] for a, b in GRID9], axis=1)
+    block_grad = flipped(same + shift_rows(dot(lhs, rhs, NT), 1, cw))
+    share = cb // (128 // cw)
+    beside = []
+    for c in range(nh):
+        groups = [block_grad[c * cb + q : c * cb + q + share, :cw] for q in range(0, cb, share)]
+        beside.append(jnp.concatenate(groups, axis=1))
+    gu_out = scatter_rows(14, swapu, pru, cb, gsu, gru, beside=beside)
+    gskip[...] = back[:, cu:].astype(BF16).reshape(2, 2, 2 * cw, cu)
+    out_gskip = pltpu.make_async_copy(gskip, gskip_hbm, loc.at[8])
+    out_gskip.start()
 
     def finish(spread, into, out, hbm, at):
         spread.wait_recv()
@@ -566,19 +578,30 @@
         copy.start()
         return copy
 
-    finished = [finish(g2_out, gr2, sumsecond, sumsecond_hbm, 9)]
-    cg_out.wait_recv()
+    finished = [finish(g2_out, gr2, sumsecond, sumsecond_hbm, 9), finish(g1_out, gr1, sumfirst, sumfirst_hbm, 12)]
+    sent = len(log) - 1
+    for part in log[:sent]:
+        part.wait_send()
+    finished.append(finish(gu_out, gru, sumup, sumup_hbm, 11))
+    base = 2 * cb // 16 * 16
+    for s in range(nh):
+        cgr[s] = gru[s, base : gru.shape[1]].astype(F32)[2 * cb - base : 2 * cb - base + cgr.shape[1]]
     out_cg = pltpu.make_async_copy(cgr, cgrows, loc.at[10])
     out_cg.start()
-    finished.append(finish(gu_out, gru, sumup, sumup_hbm, 11))
-    finished.append(finish(g1_out, gr1, sumfirst, sumfirst_hbm, 12))
     for copy in finished + [out_cg, out_result, out_gskip]:
         copy.wait()
 
-    for part in log:
+    for part in log[sent:]:
         if not part.arrived:
             part.wait_recv()
         part.wait_send()
+
+
+def tall_turn(value):
+    rows = value.shape[0]
+    if rows < 128:
+        value = jnp.concatenate([value, jnp.zeros((128 - rows, value.shape[1]), F32)], axis=0)
+    return value.T
 
 
 def closing(nh, *refs):
@@ -610,19 +633,22 @@
         arriving.wait()
         leaving.start()
     no = out3.shape[1]
-    for k, (total, out) in enumerate(((sumup, out3), (sumfirst, out4))):
-        into[1 + k].wait()
-        n = out.shape[2]
-        turned = total[...]
-        if turned.shape[0] < 128:
-            fill = jnp.zeros((128 - turned.shape[0], turned.shape[1]), F32)
-            turned = jnp.concatenate([turned, fill], axis=0)
-        out[...] = turned.T[: 27 * no, :n].reshape(27, no, n)
-        away[1 + k].start()
+    into[2].wait()
+    n = out4.shape[2]
+    out4[...] = tall_turn(sumfirst[...])[: 27 * no, :n].reshape(27, no, n)
+    away[2].start()
+    into[1].wait()
+    n = out3.shape[2]
+    turned = tall_turn(sumup[...])
+    out3[:14] = turned[: 14 * no, :n].reshape(14, no, n)
+    out3[14:] = turned[: 13 * no, n : 2 * n].reshape(13, no, n)
+    away[1].start()
     into[3].wait()
     total = sumsecond[...]
+    n = out5.shape[1]
     for t in range(27):
-        out5[t] = total[: out5.shape[1], t * no : (t + 1) * no]
+        row, at = (0, t) if t < 14 else (n, t - 14)
+        out5[t] = total[row : row + n, at * no : (at + 1) * no]
     away[3].start()
     for copy in whole + away:
         copy.wait()
@@ -644,13 +670,13 @@
     w1 = w_first.reshape(27, cj, cu)
     w2 = w_second.reshape(27, cu, cu)
     cells = rows[0] * rows[1] * fw
-    line = max(nd, nh)
     wide = round_up(cin, 128)
     part = 27 * no
     tall = round_up(cb * cw // 128, 8)
+    lanes = round_up(14 * no, 128)
     scratch = [
         v((cb, nh, cw), BF16), v(skip.shape, BF16), v(skip.shape, BF16),
-        v((round_up(cb, 8), taps), F32), v((round_up(ncj, 8), taps), F32), v((round_up(nch, 8), taps), F32),
+        v((2 * cb, lanes), F32), v((round_up(ncj, 8), taps), F32), v((2 * nch, lanes), F32),
         v(upw.shape, BF16), v(w1.shape, BF16), v(w2.shape, BF16), v(cotangent.shape, BF16),
         v((cb * nh, cw), F32),
         v((nh, round_up(cb, 16), 128), BF16), v((nh, round_up(cb, 16), 128), BF16),
@@ -670,15 +696,15 @@
         v((2, 2, fw, cu), F32),
         v((3, 3, 2, cw, cu), BF16),
         v((cu, cells), BF16), v((npair, both, cells), BF16),
-        v((nh, tall, 128), F32), v((nh, tall, 128), F32),
+        v((nh, tall, 128), F32),
         v((2 * part, cj), F32), v((2 * part, cu), F32),
         v((part, cu), F32), v((part, cu), F32),
         v((part, cj), F32), v((part, cj), F32),
         v((part, wide), F32), v((part, wide), F32),
-        v((nh, round_up(nch, 8), taps), F32), v((nh, round_up(nch, 8), taps), F32),
+        v((nh, round_up(2 * nch, 16), lanes), BF16), v((nh, round_up(2 * nch, 16), lanes), BF16),
         v((nh, round_up(ncj, 16), taps), BF16), v((nh, round_up(ncj, 16), taps), BF16),
-        v((nh, round_up(cb, 16), taps), BF16), v((nh, round_up(cb, 16), taps), BF16),
-        pltpu.SemaphoreType.DMA((18, line)), pltpu.SemaphoreType.DMA((18, line)),
+        v((nh, round_up(2 * cb + tall, 16), lanes), BF16), v((nh, round_up(2 * cb + tall, 16), lanes), BF16),
+        pltpu.SemaphoreType.DMA((18,)), pltpu.SemaphoreType.DMA((18,)),
         pltpu.SemaphoreType.DMA((6, 9)), pltpu.SemaphoreType.DMA((6, 9)),
         pltpu.SemaphoreType.DMA((13,)),
     ]
@@ -686,9 +712,9 @@
     anywhere = pl.BlockSpec(memory_space=pl.ANY)
     tops = [
         shape((nh, tall, 128), F32),
-        shape((round_up(cb, 8), taps), F32),
+        shape((2 * cb, lanes), F32),
         shape((round_up(ncj, 8), taps), F32),
-        shape((round_up(nch, 8), taps), F32),
+        shape((2 * nch, lanes), F32),
     ]
     left = pl.pallas_call(
         functools.partial(body, nd, nh, factor),

time: 83 us -> 75.6 us (0.911)
  Pallas kernels: 82.2 us -> 74.8 us
    pallas_call x1, Pallas kernels: 80.2 us -> 72.7 us  [per_device(): pl.pallas_call(functools.partial(body, nd, nh, factor), out_shape=[shape(...]
where the time goes in v5:
time: 75.6 us; the launch traced here: 75.4 us
  Pallas kernels  74.8 us (99%)
    pallas_call x1, Pallas kernels, per_device(): pl.pallas_call(functools.partial(body, nd, nh, factor), out_shape=[shape(...  72.7 us
    pallas_call x1, Pallas kernels, per_device(): pl.pallas_call(functools.partial(closing, nh), out_shape=[shape(skip.shap...  2.07 us

profile of v5, /device:TPU:1, one launch (start us, length us, event | category | flops | bytes accessed | tf_op | source)
XLA Modules:
  0.0 75.4 jit_solution(13417949585111040428)
XLA Ops:
  0.6 72.7 %decoder.1 = (bf16[2,2,64,128]{3,2,1,0:T(8,128)(2,1)}, bf16[2,2,64,128]{3,2,1,0:T(8,128)(2,1)}, f32[16,8,128]{2,1,0:T(8,128)}, f32[40,128]{1,0:T(8,128)}, f32[16,256]{1,0:T(8,128)}, /*index=5*/f32[16,128]{1,0:T(8,128)}) custom-call(bf16[20,16,32]{2,1,0:T(8,128)(2,1)} %bitcast.20, bf16[2,2,64,128]{3,2,1,0:T(8,128)(2,1)} %skip.1, ...), custom_call_target="tpu_custom_call" | custom-call | tf_op jit(solution)/shard_map/decoder/pallas_call | solution.py:719
  73.4 2.1 %closing.1 = (bf16[2,2,64,128]{3,2,1,0:T(8,128)(2,1)}, bf16[20,16,32]{2,1,0:T(8,128)(2,1)}, bf16[2,2,64,128]{3,2,1,0:T(8,128)(2,1)}, f32[27,8,20]{2,1,0:T(8,128)...) custom-call(bf16[2,2,64,128]{3,2,1,0:T(8,128)(2,1)} %get-tuple-element.18.refs_0_, ...), custom_call_target="tpu_custom_call" | custom-call | tf_op jit(solution)/shard_map/closing/pallas_call | solution.py:732

commit v6 on v5

--- a/solution.py
+++ b/solution.py
@@ -122,7 +122,7 @@
     nd, nh, factor,
     bottom_hbm, skip, upw_hbm, w1_hbm, w2_hbm, cot_hbm,
     result_hbm, gskip_hbm, cgrows, sumup_hbm, sumfirst_hbm, sumsecond_hbm,
-    bottom, result, gskip, sumup, sumfirst, sumsecond, upw, w1, w2, cot, bott, bsend, brecv, near, bg, up32, joined, ug, sg, fp, hid, hg, e2, e1, et2s, et2r, et1s, et1r,
+    bottom, result, gskip, sumup, sumfirst, sumsecond, upw, w1, w2, cot, bott, bsend, brecv, near, bg, up32, joined, ug32, ug, sg, fp, hid, hg, e2, e1, et2s, et2r, et1s, et1r,
     bu32, bu, buts, butr, cgr, acc1, acc2, px2, pr2, px1, pr1, pxu, pru, gs2, gr2, gs1, gr1, gsu, gru,
     ssem, rsem, hs, hr, loc,
 ):
@@ -361,9 +361,13 @@
     hid_halo = field_halo(2, hid)
     hid_halo.start()
     hg[pair] = hidden
-    ug[pair] = joined[1:3, 1:3, :, 0:cu].reshape(cells, cu)
-    up_out = line_p(4, lambda p: ug.at[pair], ug)
-    up_out.start()
+    hid_out = line_p(3, lambda p: hg.at[pair], hg)
+    hid_out.start()
+    planes_out.wait_recv()
+    planes_swap = single(
+        16, bg.at[core, pl.ds(0, npair)], bg.at[core, pl.ds(0, npair)], (partner, h), bg.at[1 - core, pl.ds(0, npair)]
+    )
+    planes_swap.start()
 
     weights[2].wait()
     weights[3].wait()
@@ -376,8 +380,28 @@
     out_result.start()
     e2_halo = field_halo(3, e2)
     e2_halo.start()
-    hid_out = line_p(3, lambda p: hg.at[pair], hg)
-    hid_out.start()
+
+    planes_swap.wait_recv()
+
+    def planes_of(sd, sh):
+        return bg[lax.rem(core + sd, 2), pl.ds(core * sd, npair), sh].reshape(npair * cw, wide)
+
+    taps_of = (((1, 0),), ((2, 0), (0, 1)))
+    for pd in range(2):
+        for ph in range(2):
+            total = None
+            for kd, sd in taps_of[pd]:
+                for kh, sh in taps_of[ph]:
+                    t = kd * 9 + kh * 3
+                    rhs = jnp.concatenate([upw[t], upw[t + 1], upw[t + 2]], axis=1)
+                    part = dot(planes_of(sd, sh)[:, :cin], rhs)
+                    total = part if total is None else total + part
+            even = total[:, cu : 2 * cu]
+            odd = total[:, 2 * cu :] + shift_rows(total[:, :cu], -1, cw)
+            for k in range(npair):
+                ug32[k, pd * 2 + ph, pl.ds(0, cw, stride=2), :] = even[k * cw : (k + 1) * cw]
+                ug32[k, pd * 2 + ph, pl.ds(1, cw, stride=2), :] = odd[k * cw : (k + 1) * cw]
+    ug[...] = ug32[...].astype(BF16).reshape(npair, cells, cu)
 
     def part_of(p):
         return pl.ds(pl.multiple_of(p * both, both), both)
@@ -490,14 +514,8 @@
     e2_out.wait_recv()
     hid_out.wait_recv()
     swap2 = swap(9, weight_grad(et2r, lambda j: hg[j], acc2), px2, pr2)
-    planes_out.wait_recv()
-    planes_swap = single(
-        16, bg.at[core, pl.ds(0, npair)], bg.at[core, pl.ds(0, npair)], (partner, h), bg.at[1 - core, pl.ds(0, npair)]
-    )
-    planes_swap.start()
 
     e1_out.wait_recv()
-    up_out.wait_recv()
     skip_out.wait_recv()
     swap1 = swap(13, weight_grad(et1r, lambda j: jnp.concatenate([ug[j], sg[j].reshape(cells, cu)], axis=1), acc1), px1, pr1)
 
@@ -528,15 +546,12 @@
         value = phases[PARITY_SHIFT[kd][0], PARITY_SHIFT[kh][0], pw]
         return shift_lanes(value, 1, cw) if sw else value
 
-    planes_swap.wait_recv()
     products = {}
     for sd, kds in ((0, (1, 2)), (1, (0,))):
         for sh, khs in ((0, (1, 2)), (1, (0,))):
             order = [(kd, kh, kw) for kd in kds for kh in khs for kw in range(3)]
             lhs = jnp.concatenate([tap_rows(*k) for k in order], axis=0).astype(BF16)
-            odd_one = lax.rem(core + sd, 2)
-            first = core * sd
-            rhs = bg[odd_one, pl.ds(first, npair), sh].reshape(span, -1)
+            rhs = planes_of(sd, sh)
             value = dot(lhs, rhs)
             for i, k in enumerate(order):
                 for c in range(2):
@@ -684,6 +699,7 @@
         v((2, npair + 1, 2, cw, wide), BF16),
         v((4, 4, fw, cu), F32),
         v((4, 4, fw, cj), BF16),
+        v((npair, 4, fw, cu), F32),
         v((npair, cells, cu), BF16),
         v((npair,) + skip.shape, BF16),
         v((cells, cu), F32),

time: 75.6 us -> 73 us (0.966)
  Pallas kernels: 74.8 us -> 72.3 us
    pallas_call x1, Pallas kernels: 72.7 us -> 70.2 us  [per_device(): pl.pallas_call(functools.partial(body, nd, nh, factor), out_shape=[shape(...]
where the time goes in v6:
time: 73 us; the launch traced here: 72.9 us
  Pallas kernels  72.3 us (99%)
    pallas_call x1, Pallas kernels, per_device(): pl.pallas_call(functools.partial(body, nd, nh, factor), out_shape=[shape(...  70.2 us
    pallas_call x1, Pallas kernels, per_device(): pl.pallas_call(functools.partial(closing, nh), out_shape=[shape(skip.shap...  2.07 us

profile of v6, /device:TPU:1, one launch (start us, length us, event | category | flops | bytes accessed | tf_op | source)
XLA Modules:
  0.0 72.9 jit_solution(10415992376344440623)
XLA Ops:
  0.6 70.2 %decoder.1 = (bf16[2,2,64,128]{3,2,1,0:T(8,128)(2,1)}, bf16[2,2,64,128]{3,2,1,0:T(8,128)(2,1)}, f32[16,8,128]{2,1,0:T(8,128)}, f32[40,128]{1,0:T(8,128)}, f32[16,256]{1,0:T(8,128)}, /*index=5*/f32[16,128]{1,0:T(8,128)}) custom-call(bf16[20,16,32]{2,1,0:T(8,128)(2,1)} %bitcast.20, bf16[2,2,64,128]{3,2,1,0:T(8,128)(2,1)} %skip.1, ...), custom_call_target="tpu_custom_call" | custom-call | tf_op jit(solution)/shard_map/decoder/pallas_call | solution.py:735
  70.8 2.1 %closing.1 = (bf16[2,2,64,128]{3,2,1,0:T(8,128)(2,1)}, bf16[20,16,32]{2,1,0:T(8,128)(2,1)}, bf16[2,2,64,128]{3,2,1,0:T(8,128)(2,1)}, f32[27,8,20]{2,1,0:T(8,128)...) custom-call(bf16[2,2,64,128]{3,2,1,0:T(8,128)(2,1)} %get-tuple-element.18.refs_0_, ...), custom_call_target="tpu_custom_call" | custom-call | tf_op jit(solution)/shard_map/closing/pallas_call | solution.py:748

commit v7 on v6

--- a/solution.py
+++ b/solution.py
@@ -449,7 +449,11 @@
         half = 27 * no
         halves = [value[:half], value[half:]]
         mine = jnp.where(core == 0, halves[0], halves[1])
-        out[...] = jnp.where(core == 0, halves[1], halves[0])
+        theirs = jnp.where(core == 0, halves[1], halves[0])
+        fill = out.shape[0] - half
+        if fill:
+            theirs = jnp.concatenate([theirs, jnp.zeros((fill, theirs.shape[1]), F32)], axis=0)
+        out[...] = theirs.astype(BF16)
         copy = single(phase, out, into, (partner, h), into)
         copy.start()
         return copy, mine
@@ -470,7 +474,7 @@
     def scatter_rows(phase, swapped, arriving, chunk, out, into, folded=True, beside=None):
         copy, mine = swapped
         copy.wait_recv()
-        turned = flipped((mine + arriving[...]) * factor)
+        turned = flipped((mine + arriving[...].astype(F32)[: mine.shape[0]]) * factor)
         for c in range(nh):
             piece = turned[c * chunk : (c + 1) * chunk]
             if folded:
@@ -714,9 +718,9 @@
         v((cu, cells), BF16), v((npair, both, cells), BF16),
         v((nh, tall, 128), F32),
         v((2 * part, cj), F32), v((2 * part, cu), F32),
-        v((part, cu), F32), v((part, cu), F32),
-        v((part, cj), F32), v((part, cj), F32),
-        v((part, wide), F32), v((part, wide), F32),
+        v((round_up(part, 16), cu), BF16), v((round_up(part, 16), cu), BF16),
+        v((round_up(part, 16), cj), BF16), v((round_up(part, 16), cj), BF16),
+        v((round_up(part, 16), wide), BF16), v((round_up(part, 16), wide), BF16),
         v((nh, round_up(2 * nch, 16), lanes), BF16), v((nh, round_up(2 * nch, 16), lanes), BF16),
         v((nh, round_up(ncj, 16), taps), BF16), v((nh, round_up(ncj, 16), taps), BF16),
         v((nh, round_up(2 * cb + tall, 16), lanes), BF16), v((nh, round_up(2 * cb + tall, 16), lanes), BF16),

time: 73 us -> 73 us (level)
  no operation moved by 1% of the time
where the time goes in v7:
time: 73 us; the launch traced here: 72.8 us
  Pallas kernels  72.2 us (99%)
    pallas_call x1, Pallas kernels, per_device(): pl.pallas_call(functools.partial(body, nd, nh, factor), out_shape=[shape(...  70.1 us
    pallas_call x1, Pallas kernels, per_device(): pl.pallas_call(functools.partial(closing, nh), out_shape=[shape(skip.shap...  2.07 us

profile of v7, /device:TPU:1, one launch (start us, length us, event | category | flops | bytes accessed | tf_op | source)
XLA Modules:
  0.0 72.8 jit_solution(2809827637637202670)
XLA Ops:
  0.6 70.1 %decoder.1 = (bf16[2,2,64,128]{3,2,1,0:T(8,128)(2,1)}, bf16[2,2,64,128]{3,2,1,0:T(8,128)(2,1)}, f32[16,8,128]{2,1,0:T(8,128)}, f32[40,128]{1,0:T(8,128)}, f32[16,256]{1,0:T(8,128)}, /*index=5*/f32[16,128]{1,0:T(8,128)}) custom-call(bf16[20,16,32]{2,1,0:T(8,128)(2,1)} %bitcast.20, bf16[2,2,64,128]{3,2,1,0:T(8,128)(2,1)} %skip.1, ...), custom_call_target="tpu_custom_call" | custom-call | tf_op jit(solution)/shard_map/decoder/pallas_call | solution.py:739
  70.8 2.1 %closing.1 = (bf16[2,2,64,128]{3,2,1,0:T(8,128)(2,1)}, bf16[20,16,32]{2,1,0:T(8,128)(2,1)}, bf16[2,2,64,128]{3,2,1,0:T(8,128)(2,1)}, f32[27,8,20]{2,1,0:T(8,128)...) custom-call(bf16[2,2,64,128]{3,2,1,0:T(8,128)(2,1)} %get-tuple-element.18.refs_0_, ...), custom_call_target="tpu_custom_call" | custom-call | tf_op jit(solution)/shard_map/closing/pallas_call | solution.py:752
